TPU v7x, 32 devices: a whole 2x2x4 slice. The times are simulated.
32 devices in a mesh: groups: 2 (over x), aa: 8 (over z, y), ba: 2 (over core).
Axes of the slice: x: 2, y: 2, z: 4, core: 2. Of those that a mesh axis runs over, the one named last changes fastest.
Arguments:
- video: bfloat16 [128, 8, 32, 512], P('groups', 'aa', 'ba'), parts along dimension 0, may hold values from -6 to 6
- norm_gain: float32 [3, 512], replicated, may hold values from 0.1 to 1.9
- qkv_weight: bfloat16 [3, 512, 1536], replicated, may hold values from -8 to 8
- out_weight: bfloat16 [3, 512, 512], replicated, may hold values from -0.25 to 0.25
Outputs:
- result: bfloat16 [128, 8, 32, 512], P('groups', 'aa', 'ba'), parts along dimension 0
There are 2 independent parts, one for each index of `groups`. A program takes and returns all parts, laid end to end along the dimension named above; an argument that names none is the same for every part. Nothing has to cross between parts.
All inputs are finite; a program needn't handle non-finite values.
Results may differ from a plain program's by a relative error of at most 0.014.
Values may be sent and summed in bfloat16 or wider, within the bound.
A program may use at most 64 MiB of HBM per device.

v0:
```python
import math

import jax
import jax.numpy as jnp
from jax import lax
from jax.sharding import PartitionSpec as P

HEADS = 8
HEAD_DIM = 64


score_forms = ("sbcnd,tbcnd->bcnst", "ascnd,atcnd->acnst", "absnd,abtnd->abnst")
mix_forms = ("bcnst,tbcnd->sbcnd", "acnst,atcnd->ascnd", "abnst,abtnd->absnd")


def attend(queries, key_rows, value_rows, line):
    shape = queries.shape
    split = shape[:3] + (HEADS, HEAD_DIM)
    scores = jnp.einsum(
        score_forms[line],
        queries.reshape(split),
        key_rows.reshape(split),
        preferred_element_type=jnp.float32,
    ) * (1.0 / math.sqrt(HEAD_DIM))
    weights = jax.nn.softmax(scores, axis=-1).astype(jnp.bfloat16)
    mixed = jnp.einsum(
        mix_forms[line], weights, value_rows.reshape(split), preferred_element_type=jnp.float32
    )
    return mixed.astype(jnp.bfloat16).reshape(shape)


def project_in(state, gain, weight_in):
    floats = state.astype(jnp.float32)
    meansq = jnp.mean(floats * floats, axis=-1, keepdims=True)
    normed = (floats * lax.rsqrt(meansq + 1e-06) * gain).astype(jnp.bfloat16)
    packed = jnp.dot(normed, weight_in, preferred_element_type=jnp.float32).astype(jnp.bfloat16)
    width = state.shape[-1]
    return (packed[..., :width], packed[..., width : 2 * width], packed[..., 2 * width :])


def project_out(state, mixed, weight_out):
    update = jnp.dot(mixed, weight_out, preferred_element_type=jnp.float32)
    return (state.astype(jnp.float32) + update).astype(jnp.bfloat16)


def full_block(state, gain, weight_in, weight_out, line):
    queries, key_rows, value_rows = project_in(state, gain, weight_in)
    return project_out(state, attend(queries, key_rows, value_rows, line), weight_out)


def body(video, norm_gain, qkv_weight, out_weight):
    state = full_block(video, norm_gain[0], qkv_weight[0], out_weight[0], 0)
    state = (lambda piece: full_block(piece, norm_gain[1], qkv_weight[1], out_weight[1], 1))(
        lax.all_to_all(state, "aa", split_axis=0, concat_axis=1, tiled=True)
    )
    state = (lambda piece: full_block(piece, norm_gain[2], qkv_weight[2], out_weight[2], 2))(
        lax.all_to_all(state, "ba", split_axis=1, concat_axis=2, tiled=True)
    )
    state = lax.all_to_all(
        lax.all_to_all(state, "ba", split_axis=2, concat_axis=1, tiled=True),
        "aa",
        split_axis=1,
        concat_axis=0,
        tiled=True,
    )
    return state


def solution(mesh):
    return jax.shard_map(
        body,
        mesh=mesh,
        in_specs=(P("groups", "aa", "ba", None), P(), P(), P()),
        out_specs=P("groups", "aa", "ba", None),
        check_vma=False,
    )
```

profile of v0, /device:TPU:0, one launch (start us, length us, event | category | flops | bytes accessed | tf_op | source)
XLA Modules:
  0.0 167.1 jit_solution(4037940367965702583)
XLA Ops:
  0.0 0.8 fusion.78
  0.8 1.5 fusion.13
  2.3 3.6 %fusion.6 = bf16[64,1,16,1536]{3,2,0,1:T(8,128)(2,1)S(1)} fusion(bf16[3,512,1536]{2,1,0:T(8,128)(2,1)} %param.6, bf16[64,1,16,512]{3,2,1,0:T(8,128)(2,1)} %param.4, f32[512]{0:T(512)S(1)} %bitcast.162, f32[64,16]{1,0:T(8,128)S(1)} %add_rsqrt_fusion.2), kind=kOutput, calls=%fused_computation.18 | convolution fusion | flops 1614282752 | bytes 5773312 | tf_op jit(solution)/shard_map/dot_general | solution.py:36
  5.9 1.7 %fusion.77 = (bf16[64,1,16,512]{3,2,0,1:T(8,128)(2,1)}, bf16[64,1,16,512]{3,2,0,1:T(8,128)(2,1)}, bf16[64,1,16,512]{3,2,0,1:T(8,128)(2,1)S(1)}) fusion(bf16[64,1,16,1536]{3,2,0,1:T(8,128)(2,1)S(1)} %fusion.6), kind=kLoop, calls=%fused_computation.91 | loop fusion | bytes 6291456 | tf_op jit(solution)/shard_map/slice | solution.py:38
  7.6 2.8 %reshape.130 = bf16[64,16,8,64]{3,2,1,0:T(8,128)(2,1)S(1)} reshape(bf16[64,1,16,512]{3,2,0,1:T(8,128)(2,1)} %get-tuple-element.11) | data formatting | bytes 2097152 | tf_op jit(solution)/shard_map/reshape.4
  10.4 3.9 %reshape.131 = bf16[64,16,8,64]{3,2,1,0:T(8,128)(2,1)} reshape(bf16[64,1,16,512]{3,2,0,1:T(8,128)(2,1)} %get-tuple-element.12) | data formatting | bytes 2097152 | tf_op jit(solution)/shard_map/reshape.5
  14.3 4.1 %fusion.36 = f32[16,8,64,64]{2,3,1,0:T(8,128)S(1)} fusion(bf16[64,16,8,64]{3,2,1,0:T(8,128)(2,1)} %reshape.131, bf16[64,16,8,64]{3,2,1,0:T(8,128)(2,1)S(1)} %reshape.130), kind=kOutput, calls=%fused_computation.51 | convolution fusion | flops 67108864 | bytes 4194304 | tf_op jit(solution)/shard_map/sbcnd,tbcnd->bcnst/dot_general | solution.py:19
  18.5 3.1 %fusion.79 = (f32[16,8,64]{2,1,0:T(8,128)S(1)}, f32[16,8,64,64]{2,3,1,0:T(8,128)}) fusion(f32[16,8,64,64]{2,3,1,0:T(8,128)S(1)} %fusion.36), kind=kOutput, calls=%fused_computation.93 | output fusion | flops 2097215 | bytes 4227072 | tf_op jit(solution)/shard_map/sub | solution.py:25
  21.6 1.4 copy.119
  23.0 4.2 %fusion.47 = bf16[16,8,64,64]{3,2,1,0:T(8,128)(2,1)} fusion(bf16[64,16,8,64]{0,3,2,1:T(8,128)(2,1)S(1)} %bitcast.157, f32[16,8,64,64]{2,3,1,0:T(8,128)} %get-tuple-element.18, f32[16,8,64]{2,1,0:T(8,128)S(1)} %get-tuple-element.17), kind=kOutput, calls=%fused_computation.62 | convolution fusion | flops 68681728 | bytes 4227072 | tf_op jit(solution)/shard_map/bcnst,tbcnd->sbcnd/dot_general | solution.py:26
  27.2 0.0 copy-start.3
  27.2 2.7 %copy.91 = bf16[64,16,512]{2,1,0:T(8,128)(2,1)S(1)} copy(bf16[64,16,512]{0,2,1:T(8,128)(2,1)} %bitcast.158) | data formatting | bytes 2097152 | tf_op jit(solution)/shard_map/reshape.24
  29.9 0.0 copy-done.3
  29.9 1.7 %fusion.56 = bf16[64,1,16,512]{3,2,1,0:T(8,128)(2,1)S(1)} fusion(bf16[64,16,512]{2,1,0:T(8,128)(2,1)S(1)} %copy.91, bf16[64,1,16,512]{3,2,1,0:T(8,128)(2,1)S(1)} %copy-done.3, bf16[3,512,512]{2,1,0:T(8,128)(2,1)} %param.7), kind=kOutput, calls=%fused_computation.69 | convolution fusion | flops 538443776 | bytes 3670016 | tf_op jit(solution)/shard_map/dot_general | solution.py:42
  31.7 32.8 %all_to_all.54 = bf16[64,1,16,512]{3,2,1,0:T(8,128)(2,1)S(1)} all-to-all(bf16[64,1,16,512]{3,2,1,0:T(8,128)(2,1)S(1)} %fusion.56), channel_id=1, replica_groups=mesh['groups'=2,'aa'=8,'ba'=2] {'aa'}, dimensions={0} | all-to-all | bytes 2097152 | tf_op jit(solution)/shard_map/all_to_all | solution.py:54
  64.5 0.3 fusion.24
  64.8 3.3 %convolution_convert_fusion.1 = bf16[8,8,16,1536]{3,2,1,0:T(8,128)(2,1)S(1)} fusion(bf16[3,512,1536]{2,1,0:T(8,128)(2,1)} %param.6, f32[512]{0:T(512)S(1)} %bitcast.161, f32[8,8,16]{2,1,0:T(8,128)S(1)} %add_rsqrt_fusion.1, bf16[8,8,1,16,512]{4,3,1,0,2:T(8,128)(2,1)S(1)} %bitcast.152), kind=kOutput, calls=%fused_computation.10 | convolution fusion | flops 1614282752 | bytes 5773312 | tf_op jit(solution)/shard_map/dot_general | solution.py:36
  68.1 1.8 %fusion.76 = (bf16[8,8,16,512]{3,2,1,0:T(8,128)(2,1)}, bf16[8,8,16,512]{3,2,1,0:T(8,128)(2,1)}, bf16[8,8,16,512]{3,2,1,0:T(8,128)(2,1)}) fusion(bf16[8,8,16,1536]{3,2,1,0:T(8,128)(2,1)S(1)} %convolution_convert_fusion.1), kind=kLoop, calls=%fused_computation.90 | loop fusion | bytes 6291456 | tf_op jit(solution)/shard_map/slice | solution.py:38
  69.9 2.8 %reshape.134 = bf16[8,8,16,8,64]{4,3,2,1,0:T(8,128)(2,1)S(1)} reshape(bf16[8,8,16,512]{3,2,1,0:T(8,128)(2,1)} %get-tuple-element.10) | data formatting | bytes 2097152 | tf_op jit(solution)/shard_map/reshape | solution.py:21
  72.7 3.9 %reshape.135 = bf16[8,8,16,8,64]{4,3,2,1,0:T(8,128)(2,1)} reshape(bf16[8,8,16,512]{3,2,1,0:T(8,128)(2,1)} %get-tuple-element.9) | data formatting | bytes 2097152 | tf_op jit(solution)/shard_map/reshape | solution.py:22
  76.6 4.1 %fusion.33 = f32[8,16,8,8,8]{3,4,2,1,0:T(8,128)S(1)} fusion(bf16[8,8,16,8,64]{4,3,2,1,0:T(8,128)(2,1)} %reshape.135, bf16[8,8,16,8,64]{4,3,2,1,0:T(8,128)(2,1)S(1)} %reshape.134), kind=kOutput, calls=%fused_computation.48 | convolution fusion | flops 8388608 | bytes 2359296 | tf_op jit(solution)/shard_map/ascnd,atcnd->acnst/dot_general | solution.py:19
  80.7 0.0 copy-start
  80.7 3.8 %fusion.80 = (f32[8,16,8,8]{3,2,1,0:T(8,128)S(1)}, f32[8,16,8,8,8]{3,4,2,1,0:T(8,128)}) fusion(f32[8,16,8,8,8]{3,4,2,1,0:T(8,128)S(1)} %fusion.33), kind=kOutput, calls=%fused_computation.94 | output fusion | flops 262151 | bytes 557056 | tf_op jit(solution)/shard_map/sub | solution.py:25
  84.5 0.0 copy-done
  84.5 2.1 %reshape.133 = bf16[8,8,16,8,64]{4,3,2,1,0:T(8,128)(2,1)} reshape(bf16[8,8,16,512]{3,2,1,0:T(8,128)(2,1)S(1)} %copy-done) | data formatting | bytes 2097152 | tf_op jit(solution)/shard_map/reshape | solution.py:27
  86.6 4.1 %convert_bitcast_fusion.1 = bf16[8,8,16,8,64]{4,1,3,2,0:T(8,128)(2,1)S(1)} fusion(f32[8,16,8,8,8]{3,4,2,1,0:T(8,128)} %get-tuple-element.20, f32[8,16,8,8]{3,2,1,0:T(8,128)S(1)} %get-tuple-element.19, bf16[8,8,16,8,64]{4,3,2,1,0:T(8,128)(2,1)} %reshape.133), kind=kOutput, calls=%fused_computation.57 | convolution fusion | flops 9043968 | bytes 2392064 | tf_op jit(solution)/shard_map/acnst,atcnd->ascnd/dot_general | solution.py:26
  90.7 0.6 copy.99
  91.3 2.0 %reshape.136 = bf16[8,8,16,512]{3,2,1,0:T(8,128)(2,1)} reshape(bf16[8,8,16,8,64]{4,3,2,1,0:T(8,128)(2,1)S(1)} %copy.99) | data formatting | bytes 2097152 | tf_op jit(solution)/shard_map/reshape | solution.py:29
  93.3 2.1 %fusion.25 = bf16[8,8,16,512]{3,2,1,0:T(8,128)(2,1)S(1)} fusion(bf16[8,8,16,512]{3,2,1,0:T(8,128)(2,1)} %reshape.136, bf16[3,512,512]{2,1,0:T(8,128)(2,1)} %param.7, bf16[8,8,1,16,512]{4,3,1,0,2:T(8,128)(2,1)S(1)} %bitcast.153), kind=kOutput, calls=%fused_computation.39 | convolution fusion | flops 538443776 | bytes 3670016 | tf_op jit(solution)/shard_map/dot_general | solution.py:42
  95.4 0.1 copy.100
  95.5 4.6 %all_to_all.55 = bf16[8,8,16,512]{3,2,0,1:T(8,128)(2,1)S(1)} all-to-all(bf16[8,8,16,512]{3,2,0,1:T(8,128)(2,1)S(1)} %copy.100), channel_id=1, replica_groups=mesh['groups'=2,'aa'=8,'ba'=2] {'ba'}, dimensions={1} | all-to-all | bytes 2097152 | tf_op jit(solution)/shard_map/all_to_all | solution.py:57
  100.1 0.3 bitcast_convert_fusion
  100.3 0.3 fusion.23
  100.6 0.3 fusion.22
  100.9 3.2 %convolution_convert_fusion = bf16[8,4,32,1536]{3,2,1,0:T(8,128)(2,1)S(1)} fusion(bf16[8,4,32,512]{3,2,1,0:T(8,128)(2,1)S(1)} %bitcast.159, bf16[3,512,1536]{2,1,0:T(8,128)(2,1)} %param.6), kind=kOutput, calls=%fused_computation.9 | convolution fusion | flops 1612185600 | bytes 5767168 | tf_op jit(solution)/shard_map/dot_general | solution.py:36
  104.2 1.7 %fusion.75 = (bf16[8,4,32,512]{3,2,1,0:T(8,128)(2,1)}, bf16[8,4,32,512]{3,2,1,0:T(8,128)(2,1)}, bf16[8,4,32,512]{3,2,1,0:T(8,128)(2,1)}) fusion(bf16[8,4,32,1536]{3,2,1,0:T(8,128)(2,1)S(1)} %convolution_convert_fusion), kind=kLoop, calls=%fused_computation.89 | loop fusion | bytes 6291456 | tf_op jit(solution)/shard_map/slice | solution.py:38
  105.9 2.8 %reshape.138 = bf16[8,4,32,8,64]{4,3,2,1,0:T(8,128)(2,1)S(1)} reshape(bf16[8,4,32,512]{3,2,1,0:T(8,128)(2,1)} %get-tuple-element.7) | data formatting | bytes 2097152 | tf_op jit(solution)/shard_map/reshape | solution.py:21
  108.7 3.9 %reshape.139 = bf16[8,4,32,8,64]{4,3,2,1,0:T(8,128)(2,1)} reshape(bf16[8,4,32,512]{3,2,1,0:T(8,128)(2,1)} %get-tuple-element.6) | data formatting | bytes 2097152 | tf_op jit(solution)/shard_map/reshape | solution.py:22
  112.6 2.8 %fusion.29 = f32[8,4,8,32,32]{3,4,2,1,0:T(8,128)S(1)} fusion(bf16[8,4,32,8,64]{4,3,2,1,0:T(8,128)(2,1)} %reshape.139, bf16[8,4,32,8,64]{4,3,2,1,0:T(8,128)(2,1)S(1)} %reshape.138), kind=kOutput, calls=%fused_computation.44 | convolution fusion | flops 33554432 | bytes 3145728 | tf_op jit(solution)/shard_map/absnd,abtnd->abnst/dot_general | solution.py:19
  115.4 0.0 copy-start.1
  115.4 3.2 %fusion.81 = (f32[8,4,8,32]{3,2,1,0:T(8,128)S(1)}, f32[8,4,8,32,32]{3,4,2,1,0:T(8,128)}) fusion(f32[8,4,8,32,32]{3,4,2,1,0:T(8,128)S(1)} %fusion.29), kind=kOutput, calls=%fused_computation.95 | output fusion | flops 1048607 | bytes 2129920 | tf_op jit(solution)/shard_map/sub | solution.py:25
  118.7 0.0 copy-done.1
  118.7 2.1 %reshape.137 = bf16[8,4,32,8,64]{4,3,2,1,0:T(8,128)(2,1)} reshape(bf16[8,4,32,512]{3,2,1,0:T(8,128)(2,1)S(1)} %copy-done.1) | data formatting | bytes 2097152 | tf_op jit(solution)/shard_map/reshape | solution.py:27
  120.8 3.7 %convert_bitcast_fusion = bf16[8,4,32,8,64]{4,2,3,1,0:T(8,128)(2,1)S(1)} fusion(f32[8,4,8,32,32]{3,4,2,1,0:T(8,128)} %get-tuple-element.22, f32[8,4,8,32]{3,2,1,0:T(8,128)S(1)} %get-tuple-element.21, bf16[8,4,32,8,64]{4,3,2,1,0:T(8,128)(2,1)} %reshape.137), kind=kOutput, calls=%fused_computation.54 | convolution fusion | flops 34603008 | bytes 3178496 | tf_op jit(solution)/shard_map/abnst,abtnd->absnd/dot_general | solution.py:26
  124.5 1.0 copy.106
  125.5 2.0 %reshape.140 = bf16[8,4,32,512]{3,2,1,0:T(8,128)(2,1)} reshape(bf16[8,4,32,8,64]{4,3,2,1,0:T(8,128)(2,1)S(1)} %copy.106) | data formatting | bytes 2097152 | tf_op jit(solution)/shard_map/reshape | solution.py:29
  127.6 0.0 copy-start.2
  127.6 0.3 copy.101
  127.8 0.9 copy-done.2
  128.8 1.8 %fusion.20 = bf16[8,4,32,512]{3,2,1,0:T(8,128)(2,1)S(1)} fusion(f32[8,2,4,16,512]{4,3,1,2,0:T(8,128)S(1)} %copy.101, bf16[8,4,32,512]{3,2,1,0:T(8,128)(2,1)S(1)} %copy-done.2, bf16[3,512,512]{2,1,0:T(8,128)(2,1)} %param.7), kind=kOutput, calls=%fused_computation.30 | convolution fusion | flops 537919488 | bytes 4718592 | tf_op jit(solution)/shard_map/dot_general | solution.py:42
  130.5 0.8 copy.107
  131.4 4.6 %all_to_all.56 = bf16[8,4,32,512]{3,1,0,2:T(4,128)(2,1)S(1)} all-to-all(bf16[8,4,32,512]{3,1,0,2:T(4,128)(2,1)S(1)} %copy.107), channel_id=1, replica_groups=mesh['groups'=2,'aa'=8,'ba'=2] {'ba'}, dimensions={2} | all-to-all | bytes 2097152 | tf_op jit(solution)/shard_map/all_to_all | solution.py:60
  135.9 0.6 copy.108
  136.5 0.1 copy.109
  136.6 0.1 copy.110
  136.7 29.4 %all_to_all.57 = bf16[8,8,16,512]{3,2,0,1:T(8,128)(2,1)S(1)} all-to-all(bf16[8,8,16,512]{3,2,0,1:T(8,128)(2,1)S(1)} %copy.110), channel_id=1, replica_groups=mesh['groups'=2,'aa'=8,'ba'=2] {'aa'}, dimensions={1} | all-to-all | bytes 2097152 | tf_op jit(solution)/shard_map/all_to_all | solution.py:59
  166.1 1.0 copy.149
  (3 shorter events, 0.1 us)
Async XLA Ops:
  27.2 2.8 %copy-start.3 = (bf16[64,1,16,512]{3,2,1,0:T(8,128)(2,1)S(1)}, bf16[64,1,16,512]{3,2,1,0:T(8,128)(2,1)}, u32[]{:S(2)}) copy-start(bf16[64,1,16,512]{3,2,1,0:T(8,128)(2,1)} %param.4) | copy-start | bytes 3145732
  80.7 3.8 %copy-start = (bf16[8,8,16,512]{3,2,1,0:T(8,128)(2,1)S(1)}, bf16[8,8,16,512]{3,2,1,0:T(8,128)(2,1)}, u32[]{:S(2)}) copy-start(bf16[8,8,16,512]{3,2,1,0:T(8,128)(2,1)} %get-tuple-element.8) | copy-start | bytes 3145732
  115.4 3.2 %copy-start.1 = (bf16[8,4,32,512]{3,2,1,0:T(8,128)(2,1)S(1)}, bf16[8,4,32,512]{3,2,1,0:T(8,128)(2,1)}, u32[]{:S(2)}) copy-start(bf16[8,4,32,512]{3,2,1,0:T(8,128)(2,1)} %get-tuple-element.5) | copy-start | bytes 3145732
  127.6 1.2 copy-start.2
where the time goes:
time: 168 us; the launch traced here: 167 us
  blocking collectives  71.4 us (43%)
  local copies, waits for them, and re-layouts  44 us (26%)
  matrix products  38.7 us (23%)
  other arithmetic  12.8 us (8%)
    all_to_all x1, blocking collectives, body(): lax.all_to_all(state, 'aa', split_axis=0, concat_axis=1, tiled=True)  32.8 us
    all_to_all x1, blocking collectives, body(): lax.all_to_all(lax.all_to_all(state, 'ba', split_axis=2, concat_axis=1, t...  29.4 us
    dot_general x3, matrix products, attend(): jnp.einsum(mix_forms[line], weights, value_rows.reshape(split), preferred...  12 us
    dot_general x3, matrix products, attend(): jnp.einsum(score_forms[line], queries.reshape(split), key_rows.reshape(sp...  11 us
    another operation x4, local copies, waits for them, and re-layouts  10.9 us
    sub x3, other arithmetic, attend(): weights = jax.nn.softmax(scores, axis=-1).astype(jnp.bfloat16)  10.1 us
    dot_general x3, matrix products, project_in(): jnp.dot(normed, weight_in, preferred_element_type=jnp.float32)  10.1 us
    reshape x2, local copies, waits for them, and re-layouts, attend(): key_rows.reshape(split)  7.87 us

commit v1 on v0

v1 whole, which is shorter than its diff:
```python
import functools
import math

import jax
import jax.numpy as jnp
from jax import lax
from jax.experimental import pallas as pl
from jax.experimental.pallas import tpu as pltpu
from jax.sharding import PartitionSpec as P

HEADS = 8
HEAD_DIM = 64
PIECE = 16
GROUP = 128
LANES = 128
MESH = pl.DeviceIdType.MESH


score_forms = ("sbcnd,tbcnd->bcnst", "ascnd,atcnd->acnst", "absnd,abtnd->abnst")
mix_forms = ("bcnst,tbcnd->sbcnd", "acnst,atcnd->ascnd", "abnst,abtnd->absnd")


def attend(queries, key_rows, value_rows, line):
    shape = queries.shape
    split = shape[:3] + (HEADS, HEAD_DIM)
    scores = jnp.einsum(
        score_forms[line],
        queries.reshape(split),
        key_rows.reshape(split),
        preferred_element_type=jnp.float32,
    ) * (1.0 / math.sqrt(HEAD_DIM))
    weights = jax.nn.softmax(scores, axis=-1).astype(jnp.bfloat16)
    mixed = jnp.einsum(
        mix_forms[line], weights, value_rows.reshape(split), preferred_element_type=jnp.float32
    )
    return mixed.astype(jnp.bfloat16).reshape(shape)


def full_block(state, gain, weight_in, weight_out, line):
    floats = state.astype(jnp.float32)
    meansq = jnp.mean(floats * floats, axis=-1, keepdims=True)
    normed = (floats * lax.rsqrt(meansq + 1e-06) * gain).astype(jnp.bfloat16)
    packed = jnp.dot(normed, weight_in, preferred_element_type=jnp.float32).astype(jnp.bfloat16)
    width = state.shape[-1]
    mixed = attend(packed[..., :width], packed[..., width : 2 * width], packed[..., 2 * width :], line)
    update = jnp.dot(mixed, weight_out, preferred_element_type=jnp.float32)
    return (floats + update).astype(jnp.bfloat16)


def general_body(video, norm_gain, qkv_weight, out_weight):
    state = full_block(video, norm_gain[0], qkv_weight[0], out_weight[0], 0)
    state = lax.all_to_all(state, "aa", split_axis=0, concat_axis=1, tiled=True)
    state = full_block(state, norm_gain[1], qkv_weight[1], out_weight[1], 1)
    state = lax.all_to_all(state, "ba", split_axis=1, concat_axis=2, tiled=True)
    state = full_block(state, norm_gain[2], qkv_weight[2], out_weight[2], 2)
    state = lax.all_to_all(state, "ba", split_axis=2, concat_axis=1, tiled=True)
    return lax.all_to_all(state, "aa", split_axis=1, concat_axis=0, tiled=True)


def block_on(x, gain, w_in, w_out, line_of):
    tokens, d = x.shape
    meansq = jnp.mean(x * x, axis=-1, keepdims=True)
    normed = (x * lax.rsqrt(meansq + 1e-06) * gain).astype(jnp.bfloat16)
    packed = jnp.dot(normed, w_in, preferred_element_type=jnp.float32)

    pair = 2 * HEAD_DIM
    lane = lax.broadcasted_iota(jnp.int32, (GROUP, pair), 1)
    low = lane < HEAD_DIM
    scale = 1.0 / math.sqrt(HEAD_DIM)
    keep_low = jnp.where(low, scale, 0.0)
    keep_high = jnp.where(low, 0.0, scale)
    rows = line_of(lax.broadcasted_iota(jnp.int32, (2 * GROUP, GROUP), 0) % GROUP)
    cols = line_of(lax.broadcasted_iota(jnp.int32, (2 * GROUP, GROUP), 1))
    bias = jnp.where(rows == cols, 0.0, -jnp.inf)
    ones = jnp.ones((GROUP, pair), jnp.bfloat16)

    groups = []
    for g in range(tokens // GROUP):
        at = slice(g * GROUP, (g + 1) * GROUP)
        heads = []
        for p in range(d // pair):
            q = packed[at, p * pair : (p + 1) * pair]
            k = packed[at, d + p * pair : d + (p + 1) * pair].astype(jnp.bfloat16)
            v = packed[at, 2 * d + p * pair : 2 * d + (p + 1) * pair].astype(jnp.bfloat16)
            q2 = jnp.concatenate([q * keep_low, q * keep_high], axis=0).astype(jnp.bfloat16)
            s = lax.dot_general(q2, k, (((1,), (1,)), ((), ())), preferred_element_type=jnp.float32)
            s = s + bias
            e = jnp.exp(s - jnp.max(s, axis=-1, keepdims=True)).astype(jnp.bfloat16)
            o = jnp.dot(e, jnp.concatenate([v, ones], axis=1), preferred_element_type=jnp.float32)
            o = o[:, :pair] / o[:, pair:]
            heads.append(jnp.where(low, o[:GROUP], o[GROUP:]))
        groups.append(jnp.concatenate(heads, axis=1))
    mixed = jnp.concatenate(groups, axis=0).astype(jnp.bfloat16)
    return x + jnp.dot(mixed, w_out, preferred_element_type=jnp.float32)


def load_strided(ref, start, size, stride):
    return jnp.concatenate(
        [ref[p, pl.ds(start, size, stride=stride), :] for p in range(ref.shape[0])], axis=1
    )


def kernel(
    sizes, gain_ref, x_hbm, wi_hbm, wo_hbm, out_ref,
    x_ref, wi_ref, wo_ref, x32, turned, send, recv, y1, back,
    x_sem, w_sem, send_sem, recv_sem, back_sem, out_sem, own_sem,
):
    frames, rows, cols, n, cores = sizes
    mine = frames // n
    wide = PIECE // mine
    chunks = cols // wide
    per_group = GROUP // frames
    d = x_ref.shape[-1]
    planes = d // LANES
    aa, ba = lax.axis_index("aa"), lax.axis_index("ba")
    me = aa * cores + ba

    copies = [pltpu.make_async_copy(x_hbm, x_ref, x_sem)]
    for b in range(3):
        copies.append(pltpu.make_async_copy(wi_hbm.at[b], wi_ref.at[b], w_sem.at[b, 0]))
        copies.append(pltpu.make_async_copy(wo_hbm.at[b], wo_ref.at[b], w_sem.at[b, 1]))
    for copy in copies:
        copy.start()

    def where(device):
        return {"aa": device // cores, "ba": device % cores}

    barrier = pltpu.get_barrier_semaphore()

    def greet(o, c):
        pl.semaphore_signal(
            barrier, inc=1, device_id=where(lax.rem(me + o, n)), device_id_type=MESH
        )
        return c

    lax.fori_loop(1, n, greet, 0)
    copies[0].wait()
    for p in range(planes):
        x32[p] = x_ref[:, p * LANES : (p + 1) * LANES].astype(jnp.float32)
    pl.semaphore_wait(barrier, n - 1)

    copies[1].wait()
    copies[2].wait()

    def first(k, c):
        spots = [(w, f) for w in range(wide) for f in range(mine)]
        x = jnp.concatenate(
            [load_strided(x32, f * cols + k * wide + w, n, mine * cols) for w, f in spots], axis=0
        )
        y = block_on(x, gain_ref[0:1, :], wi_ref[0], wo_ref[0], lambda i: i // frames)
        for at, (w, f) in enumerate(spots):
            for p in range(planes):
                turned[p, pl.ds(w * mine + f, n, stride=PIECE), :] = y[
                    at * n : (at + 1) * n, p * LANES : (p + 1) * LANES
                ]
        for p in range(planes):
            send[k, :, :, p * LANES : (p + 1) * LANES] = (
                turned[p].astype(jnp.bfloat16).reshape(n, PIECE, LANES)
            )
        recv[k, ba, aa] = send[k, me]

        def give(o, c):
            device = lax.rem(me + o, n)
            pltpu.make_async_remote_copy(
                src_ref=send.at[k, device], dst_ref=recv.at[k, ba, aa],
                send_sem=send_sem, recv_sem=recv_sem.at[k],
                device_id=where(device), device_id_type=MESH,
            ).start()
            return c

        lax.fori_loop(1, n, give, 0)
        return c

    lax.fori_loop(0, chunks, first, 0)

    copies[3].wait()
    copies[4].wait()

    def second(k, c):
        pltpu.make_async_copy(send.at[0, 0 : n - 1], send.at[0, 0 : n - 1], recv_sem.at[k]).wait()
        x = recv[k].reshape(n * PIECE, d).astype(jnp.float32)
        y = block_on(x, gain_ref[1:2, :], wi_ref[1], wo_ref[1], lambda i: i % PIECE)
        for at in range(n):
            place = pl.multiple_of((at * chunks + k) * PIECE, PIECE)
            for p in range(planes):
                y1[p, pl.ds(place, PIECE), :] = y[
                    at * PIECE : (at + 1) * PIECE, p * LANES : (p + 1) * LANES
                ]
        return c

    lax.fori_loop(0, chunks, second, 0)

    copies[5].wait()
    copies[6].wait()
    some = GROUP // (cores * cols)

    def third(f, c):
        parts = [
            load_strided(y1, (b * rows + r) * cols * mine + f, some * cols, mine)
            for r in range(0, rows, some)
            for b in range(cores)
        ]
        x = jnp.concatenate(parts, axis=0)
        y = block_on(x, gain_ref[2:3, :], wi_ref[2], wo_ref[2], lambda i: (i // cols) % some)
        back[f] = y.astype(jnp.bfloat16).reshape(n, cols, d)
        frame = me * mine + f

        def place(device):
            r, b = device // cores, device % cores
            return ((r // some) * cores + b) * some + r % some

        pltpu.make_async_copy(
            back.at[f, place(me)], out_ref.at[frame], own_sem.at[f]
        ).start()

        def give(o, c):
            device = lax.rem(me + o, n)
            pltpu.make_async_remote_copy(
                src_ref=back.at[f, place(device)], dst_ref=out_ref.at[frame],
                send_sem=back_sem, recv_sem=out_sem,
                device_id=where(device), device_id_type=MESH,
            ).start()
            return c

        lax.fori_loop(1, n, give, 0)
        return c

    lax.fori_loop(0, mine, third, 0)

    for f in range(mine):
        pltpu.make_async_copy(back.at[f, 0], out_ref.at[f], own_sem.at[f]).wait()
    for sem, buffer in ((send_sem, send), (back_sem, back)):
        pltpu.make_async_copy(
            buffer.at[:, 0 : n - 1], buffer.at[:, 0 : n - 1], sem
        ).wait()
    others = (n - 1) * mine
    pltpu.make_async_copy(out_ref.at[0:others], out_ref.at[0:others], out_sem).wait()


def kernel_body(sizes, video, norm_gain, qkv_weight, out_weight):
    frames, rows, cols, n, cores = sizes
    d = video.shape[-1]
    tokens = frames * cols
    planes = d // LANES
    mine = frames // n
    chunks = cols * mine // PIECE
    dma = pltpu.SemaphoreType.DMA
    result = pl.pallas_call(
        functools.partial(kernel, sizes),
        out_shape=jax.ShapeDtypeStruct((frames, cols, d), jnp.bfloat16),
        in_specs=[pl.BlockSpec(memory_space=pltpu.VMEM)] + [pl.BlockSpec(memory_space=pl.ANY)] * 3,
        out_specs=pl.BlockSpec(memory_space=pl.ANY),
        scratch_shapes=[
            pltpu.VMEM((tokens, d), jnp.bfloat16),
            pltpu.VMEM(qkv_weight.shape, jnp.bfloat16),
            pltpu.VMEM(out_weight.shape, jnp.bfloat16),
            pltpu.VMEM((planes, tokens, LANES), jnp.float32),
            pltpu.VMEM((planes, n * PIECE, LANES), jnp.float32),
            pltpu.VMEM((chunks, n, PIECE, d), jnp.bfloat16),
            pltpu.VMEM((chunks, cores, n // cores, PIECE, d), jnp.bfloat16),
            pltpu.VMEM((planes, tokens, LANES), jnp.float32),
            pltpu.VMEM((mine, n, cols, d), jnp.bfloat16),
            dma,
            dma((3, 2)),
            dma,
            dma((chunks,)),
            dma,
            dma,
            dma((mine,)),
        ],
        compiler_params=pltpu.CompilerParams(
            collective_id=0, has_side_effects=True, vmem_limit_bytes=48 * 1024 * 1024
        ),
        cost_estimate=pl.CostEstimate(
            flops=2 * tokens * d * 4 * d * 3, bytes_accessed=8 * tokens * d, transcendentals=0
        ),
    )(norm_gain, video.reshape(tokens, d), qkv_weight, out_weight)
    return result.reshape(video.shape)


def fits(frames, rows, cols, n, cores, d):
    if frames % n or n != rows * cores or d % (2 * HEAD_DIM):
        return False
    mine = frames // n
    if PIECE % mine or cols != PIECE or GROUP % frames or rows * PIECE != GROUP:
        return False
    return GROUP % (cores * cols) == 0 and (n * PIECE) % GROUP == 0


def solution(mesh):
    def body(video, norm_gain, qkv_weight, out_weight):
        frames, here, cols, d = video.shape
        cores = mesh.shape["ba"]
        rows = here * mesh.shape["aa"]
        n = mesh.shape["aa"] * cores
        if here == 1 and fits(frames, rows, cols, n, cores, d):
            sizes = (frames, rows, cols, n, cores)
            return kernel_body(sizes, video, norm_gain, qkv_weight, out_weight)
        return general_body(video, norm_gain, qkv_weight, out_weight)

    return jax.shard_map(
        body,
        mesh=mesh,
        in_specs=(P("groups", "aa", "ba", None), P(), P(), P()),
        out_specs=P("groups", "aa", "ba", None),
        check_vma=False,
    )
```

time: 168 us -> 64.3 us (0.38)
  blocking collectives: 71.4 us -> 0 us
  Pallas kernels: 0 us -> 59.8 us
  local copies, waits for them, and re-layouts: 44 us -> 4.3 us
  matrix products: 38.7 us -> 0 us
  other arithmetic: 12.8 us -> 0 us
    all_to_all x4 -> x0, blocking collectives: 71.4 us -> none  [the longest x1 32.8 us: body(): lax.all_to_all(state, 'aa', split_axis=0, concat_axis=1, tiled=True)]
    pallas_call x0 -> x1, Pallas kernels: none -> 59.8 us  [kernel_body(): pl.pallas_call(functools.partial(kernel, sizes), out_shape=jax.ShapeDtype...]
    dot_general x12 -> x0, matrix products: 38.7 us -> none  [the longest x3 12 us: attend(): jnp.einsum(mix_forms[line], weights, value_rows.reshape(split), preferred...]
    reshape x8 -> x0, local copies, waits for them, and re-layouts: 21.7 us -> none  [the longest x2 7.87 us: attend(): key_rows.reshape(split)]
    another operation x4 -> x0, local copies, waits for them, and re-layouts: 10.9 us -> none
    sub x3 -> x0, other arithmetic: 10.1 us -> none  [attend(): weights = jax.nn.softmax(scores, axis=-1).astype(jnp.bfloat16)]
    slice x4 -> x0, local copies, waits for them, and re-layouts: 5.99 us -> none  [the longest x2 3.5 us: project_in(): packed[..., 2 * width:]]
    convert_element_type x5 -> x0, local copies, waits for them, and re-layouts: 2.72 us -> none  [the longest x2 1.56 us: attend(): return mixed.astype(jnp.bfloat16).reshape(shape)]
where the time goes in v1:
time: 64.3 us; the launch traced here: 64.1 us
  Pallas kernels  59.8 us (93%)
  local copies, waits for them, and re-layouts  4.3 us (7%)
    pallas_call x1, Pallas kernels, kernel_body(): pl.pallas_call(functools.partial(kernel, sizes), out_shape=jax.ShapeDtype...  59.8 us
    unnamed x7, local copies, waits for them, and re-layouts  4.3 us

profile of v1, /device:TPU:0, one launch (start us, length us, event | category | flops | bytes accessed | tf_op | source)
XLA Modules:
  0.0 64.1 jit_solution(1812738486173622537)
XLA Ops:
  0.0 0.0 copy-start
  0.0 1.4 %copy-done = bf16[3,512,512]{2,1,0:T(8,128)(2,1)S(1)} copy-done((bf16[3,512,512]{2,1,0:T(8,128)(2,1)S(1)}, bf16[3,512,512]{2,1,0:T(8,128)(2,1)}, u32[]{:S(2)}) %copy-start) | copy-done | bytes 1572888
  1.4 0.0 copy-start.1
  1.4 1.2 %copy-done.1 = bf16[64,1,16,512]{3,2,1,0:T(8,128)(2,1)S(1)} copy-done((bf16[64,1,16,512]{3,2,1,0:T(8,128)(2,1)S(1)}, bf16[64,1,16,512]{3,2,1,0:T(8,128)(2,1)}, u32[]{:S(2)}) %copy-start.1) | copy-done | bytes 1048600
  2.6 0.0 copy-start.2
  2.6 0.7 %copy-done.2 = f32[3,512]{1,0:T(4,128)S(1)} copy-done((f32[3,512]{1,0:T(4,128)S(1)}, f32[3,512]{1,0:T(4,128)}, u32[]{:S(2)}) %copy-start.2) | copy-done | bytes 6168
  3.3 59.8 %shard_map.46 = bf16[64,16,512]{2,1,0:T(8,128)(2,1)S(1)} custom-call(f32[3,512]{1,0:T(4,128)S(1)} %copy-done.2, bf16[1024,512]{1,0:T(8,128)(2,1)S(1)} %bitcast.5, bf16[3,512,1536]{2,1,0:T(8,128)(2,1)} %wi_hbm.1, bf16[3,512,512]{2,1,0:T(8,128)(2,1)S(1)} %copy-done), custom_call_target="tpu_custom_call" | custom-call | flops 6442450944 | bytes 4194304 | tf_op jit(solution)/shard_map/pallas_call | solution.py:248
  63.1 1.0 %copy.7 = bf16[64,1,16,512]{3,2,1,0:T(8,128)(2,1)} copy(bf16[64,1,16,512]{3,2,1,0:T(8,128)(2,1)S(1)} %bitcast.4) | data formatting | bytes 2097152
Async XLA Ops:
  0.0 1.4 %copy-start = (bf16[3,512,512]{2,1,0:T(8,128)(2,1)S(1)}, bf16[3,512,512]{2,1,0:T(8,128)(2,1)}, u32[]{:S(2)}) copy-start(bf16[3,512,512]{2,1,0:T(8,128)(2,1)} %wo_hbm.1) | copy-start | bytes 4718596
  1.4 1.2 %copy-start.1 = (bf16[64,1,16,512]{3,2,1,0:T(8,128)(2,1)S(1)}, bf16[64,1,16,512]{3,2,1,0:T(8,128)(2,1)}, u32[]{:S(2)}) copy-start(bf16[64,1,16,512]{3,2,1,0:T(8,128)(2,1)} %param.4) | copy-start | bytes 3145732
  2.6 0.7 %copy-start.2 = (f32[3,512]{1,0:T(4,128)S(1)}, f32[3,512]{1,0:T(4,128)}, u32[]{:S(2)}) copy-start(f32[3,512]{1,0:T(4,128)} %gain_ref.1) | copy-start | bytes 18436

commit v2 on v1

--- a/solution.py
+++ b/solution.py
@@ -101,53 +101,89 @@
 
 
 def kernel(
-    sizes, gain_ref, x_hbm, wi_hbm, wo_hbm, out_ref,
-    x_ref, wi_ref, wo_ref, x32, turned, send, recv, y1, back,
+    sizes, gain_hbm, x_hbm, wi_hbm, wo_hbm, out_ref,
+    gain_ref, x_ref, wi_ref, wo_ref, x32, turned, late, send, recv, y1, y1_late, back,
     x_sem, w_sem, send_sem, recv_sem, back_sem, out_sem, own_sem,
 ):
     frames, rows, cols, n, cores = sizes
     mine = frames // n
     wide = PIECE // mine
-    chunks = cols // wide
-    per_group = GROUP // frames
+    half = cols // 2
+    early = half // wide
+    few = PIECE // half
     d = x_ref.shape[-1]
     planes = d // LANES
     aa, ba = lax.axis_index("aa"), lax.axis_index("ba")
     me = aa * cores + ba
 
-    copies = [pltpu.make_async_copy(x_hbm, x_ref, x_sem)]
+    x_copies = [
+        pltpu.make_async_copy(x_hbm, x_ref, x_sem.at[0]),
+        pltpu.make_async_copy(gain_hbm, gain_ref, x_sem.at[1]),
+    ]
+    w_copies = []
     for b in range(3):
-        copies.append(pltpu.make_async_copy(wi_hbm.at[b], wi_ref.at[b], w_sem.at[b, 0]))
-        copies.append(pltpu.make_async_copy(wo_hbm.at[b], wo_ref.at[b], w_sem.at[b, 1]))
-    for copy in copies:
+        w_copies.append(pltpu.make_async_copy(wi_hbm.at[b], wi_ref.at[b], w_sem.at[b, 0]))
+        w_copies.append(pltpu.make_async_copy(wo_hbm.at[b], wo_ref.at[b], w_sem.at[b, 1]))
+    for copy in x_copies + w_copies[:2]:
         copy.start()
 
     def where(device):
         return {"aa": device // cores, "ba": device % cores}
 
+    near = n // 2
+
+    def other(o):
+        side = me // near
+        side = jnp.where(o < near, 1 - side, side)
+        return side * near + lax.rem(me + o, near)
+
     barrier = pltpu.get_barrier_semaphore()
 
     def greet(o, c):
-        pl.semaphore_signal(
-            barrier, inc=1, device_id=where(lax.rem(me + o, n)), device_id_type=MESH
-        )
+        pl.semaphore_signal(barrier, inc=1, device_id=where(other(o)), device_id_type=MESH)
         return c
 
-    lax.fori_loop(1, n, greet, 0)
-    copies[0].wait()
+    def others(body):
+        def step(i, c):
+            return body(jnp.where(i < near, i, i + 1), c)
+
+        lax.fori_loop(0, n - 1, step, 0)
+
+    others(greet)
+    for copy in x_copies:
+        copy.wait()
     for p in range(planes):
         x32[p] = x_ref[:, p * LANES : (p + 1) * LANES].astype(jnp.float32)
+    for copy in w_copies[:2]:
+        copy.wait()
+    for copy in w_copies[2:]:
+        copy.start()
     pl.semaphore_wait(barrier, n - 1)
 
-    copies[1].wait()
-    copies[2].wait()
-
-    def first(k, c):
-        spots = [(w, f) for w in range(wide) for f in range(mine)]
+    spots = [(w, f) for w in range(wide) for f in range(mine)]
+
+    def along_frames(k):
         x = jnp.concatenate(
             [load_strided(x32, f * cols + k * wide + w, n, mine * cols) for w, f in spots], axis=0
         )
-        y = block_on(x, gain_ref[0:1, :], wi_ref[0], wo_ref[0], lambda i: i // frames)
+        return block_on(x, gain_ref[0:1, :], wi_ref[0], wo_ref[0], lambda i: i // frames)
+
+    def give_chunk(k):
+        recv[k, ba, aa] = send[k, me]
+
+        def give(o, c):
+            device = other(o)
+            pltpu.make_async_remote_copy(
+                src_ref=send.at[k, device], dst_ref=recv.at[k, ba, aa],
+                send_sem=send_sem, recv_sem=recv_sem.at[k],
+                device_id=where(device), device_id_type=MESH,
+            ).start()
+            return c
+
+        others(give)
+
+    def first(k, c):
+        y = along_frames(k)
         for at, (w, f) in enumerate(spots):
             for p in range(planes):
                 turned[p, pl.ds(w * mine + f, n, stride=PIECE), :] = y[
@@ -157,52 +193,68 @@
             send[k, :, :, p * LANES : (p + 1) * LANES] = (
                 turned[p].astype(jnp.bfloat16).reshape(n, PIECE, LANES)
             )
-        recv[k, ba, aa] = send[k, me]
-
-        def give(o, c):
-            device = lax.rem(me + o, n)
-            pltpu.make_async_remote_copy(
-                src_ref=send.at[k, device], dst_ref=recv.at[k, ba, aa],
-                send_sem=send_sem, recv_sem=recv_sem.at[k],
-                device_id=where(device), device_id_type=MESH,
-            ).start()
-            return c
-
-        lax.fori_loop(1, n, give, 0)
+        give_chunk(k)
         return c
 
-    lax.fori_loop(0, chunks, first, 0)
-
-    copies[3].wait()
-    copies[4].wait()
-
-    def second(k, c):
+    lax.fori_loop(0, early, first, 0)
+
+    def first_late(k, c):
+        y = along_frames(early + k)
+        for at, (w, f) in enumerate(spots):
+            row = (f // few) * n * PIECE + (k * wide + w) * few + f % few
+            for p in range(planes):
+                late[p, pl.ds(row, n, stride=PIECE), :] = y[
+                    at * n : (at + 1) * n, p * LANES : (p + 1) * LANES
+                ]
+        return c
+
+    lax.fori_loop(0, early, first_late, 0)
+    for h in range(mine // few):
+        for p in range(planes):
+            send[early + h, :, :, p * LANES : (p + 1) * LANES] = (
+                late[p, h * n * PIECE : (h + 1) * n * PIECE]
+                .astype(jnp.bfloat16)
+                .reshape(n, PIECE, LANES)
+            )
+        give_chunk(early + h)
+
+    for copy in w_copies[2:]:
+        copy.wait()
+
+    def along_rows(k):
         pltpu.make_async_copy(send.at[0, 0 : n - 1], send.at[0, 0 : n - 1], recv_sem.at[k]).wait()
         x = recv[k].reshape(n * PIECE, d).astype(jnp.float32)
-        y = block_on(x, gain_ref[1:2, :], wi_ref[1], wo_ref[1], lambda i: i % PIECE)
+        return block_on(x, gain_ref[1:2, :], wi_ref[1], wo_ref[1], lambda i: i % PIECE)
+
+    def second(k, c):
+        y = along_rows(k)
         for at in range(n):
-            place = pl.multiple_of((at * chunks + k) * PIECE, PIECE)
+            place = pl.multiple_of((at * early + k) * PIECE, PIECE)
             for p in range(planes):
                 y1[p, pl.ds(place, PIECE), :] = y[
                     at * PIECE : (at + 1) * PIECE, p * LANES : (p + 1) * LANES
                 ]
         return c
 
-    lax.fori_loop(0, chunks, second, 0)
-
-    copies[5].wait()
-    copies[6].wait()
+    lax.fori_loop(0, early, second, 0)
+
     some = GROUP // (cores * cols)
 
-    def third(f, c):
-        parts = [
-            load_strided(y1, (b * rows + r) * cols * mine + f, some * cols, mine)
-            for r in range(0, rows, some)
-            for b in range(cores)
-        ]
+    def third(h, i):
+        f = h * few + i
+        parts = []
+        for r in range(0, rows, some):
+            for b in range(cores):
+                at = b * rows + r
+                parts.append(load_strided(y1, at * half * mine + f, some * half, mine))
+                parts.append(load_strided(y1_late, at * half * few + i, some * half, few))
         x = jnp.concatenate(parts, axis=0)
-        y = block_on(x, gain_ref[2:3, :], wi_ref[2], wo_ref[2], lambda i: (i // cols) % some)
-        back[f] = y.astype(jnp.bfloat16).reshape(n, cols, d)
+        y = block_on(x, gain_ref[2:3, :], wi_ref[2], wo_ref[2], lambda t: (t // half) % some)
+        for at in range(n):
+            low = (at // some) * 2 * some * half + (at % some) * half
+            high = low + some * half
+            piece = jnp.concatenate([y[low : low + half], y[high : high + half]], axis=0)
+            back[f, at] = piece.astype(jnp.bfloat16)
         frame = me * mine + f
 
         def place(device):
@@ -214,7 +266,7 @@
         ).start()
 
         def give(o, c):
-            device = lax.rem(me + o, n)
+            device = other(o)
             pltpu.make_async_remote_copy(
                 src_ref=back.at[f, place(device)], dst_ref=out_ref.at[frame],
                 send_sem=back_sem, recv_sem=out_sem,
@@ -222,10 +274,20 @@
             ).start()
             return c
 
-        lax.fori_loop(1, n, give, 0)
-        return c
-
-    lax.fori_loop(0, mine, third, 0)
+        others(give)
+
+    def rest(h, c):
+        y = along_rows(early + h)
+        for p in range(planes):
+            y1_late[p] = y[:, p * LANES : (p + 1) * LANES]
+
+        def frame_of(i, c):
+            third(h, i)
+            return c
+
+        return lax.fori_loop(0, few, frame_of, c)
+
+    lax.fori_loop(0, mine // few, rest, 0)
 
     for f in range(mine):
         pltpu.make_async_copy(back.at[f, 0], out_ref.at[f], own_sem.at[f]).wait()
@@ -233,8 +295,8 @@
         pltpu.make_async_copy(
             buffer.at[:, 0 : n - 1], buffer.at[:, 0 : n - 1], sem
         ).wait()
-    others = (n - 1) * mine
-    pltpu.make_async_copy(out_ref.at[0:others], out_ref.at[0:others], out_sem).wait()
+    total = (n - 1) * mine
+    pltpu.make_async_copy(out_ref.at[0:total], out_ref.at[0:total], out_sem).wait()
 
 
 def kernel_body(sizes, video, norm_gain, qkv_weight, out_weight):
@@ -248,19 +310,22 @@
     result = pl.pallas_call(
         functools.partial(kernel, sizes),
         out_shape=jax.ShapeDtypeStruct((frames, cols, d), jnp.bfloat16),
-        in_specs=[pl.BlockSpec(memory_space=pltpu.VMEM)] + [pl.BlockSpec(memory_space=pl.ANY)] * 3,
+        in_specs=[pl.BlockSpec(memory_space=pltpu.HBM)] * 4,
         out_specs=pl.BlockSpec(memory_space=pl.ANY),
         scratch_shapes=[
+            pltpu.VMEM(norm_gain.shape, jnp.float32),
             pltpu.VMEM((tokens, d), jnp.bfloat16),
             pltpu.VMEM(qkv_weight.shape, jnp.bfloat16),
             pltpu.VMEM(out_weight.shape, jnp.bfloat16),
             pltpu.VMEM((planes, tokens, LANES), jnp.float32),
             pltpu.VMEM((planes, n * PIECE, LANES), jnp.float32),
+            pltpu.VMEM((planes, tokens // 2, LANES), jnp.float32),
             pltpu.VMEM((chunks, n, PIECE, d), jnp.bfloat16),
             pltpu.VMEM((chunks, cores, n // cores, PIECE, d), jnp.bfloat16),
-            pltpu.VMEM((planes, tokens, LANES), jnp.float32),
+            pltpu.VMEM((planes, tokens // 2, LANES), jnp.float32),
+            pltpu.VMEM((planes, n * PIECE, LANES), jnp.float32),
             pltpu.VMEM((mine, n, cols, d), jnp.bfloat16),
-            dma,
+            dma((2,)),
             dma((3, 2)),
             dma,
             dma((chunks,)),
@@ -269,7 +334,7 @@
             dma((mine,)),
         ],
         compiler_params=pltpu.CompilerParams(
-            collective_id=0, has_side_effects=True, vmem_limit_bytes=48 * 1024 * 1024
+            collective_id=0, has_side_effects=True, vmem_limit_bytes=62 * 1024 * 1024
         ),
         cost_estimate=pl.CostEstimate(
             flops=2 * tokens * d * 4 * d * 3, bytes_accessed=8 * tokens * d, transcendentals=0
@@ -279,10 +344,13 @@
 
 
 def fits(frames, rows, cols, n, cores, d):
-    if frames % n or n != rows * cores or d % (2 * HEAD_DIM):
+    if frames % n or n != rows * cores or n % 2 or d % (2 * HEAD_DIM):
         return False
     mine = frames // n
     if PIECE % mine or cols != PIECE or GROUP % frames or rows * PIECE != GROUP:
+        return False
+    half = cols // 2
+    if half % (PIECE // mine) or mine % (PIECE // half):
         return False
     return GROUP % (cores * cols) == 0 and (n * PIECE) % GROUP == 0
 

time: 64.3 us -> 61.6 us (0.958)
  local copies, waits for them, and re-layouts: 4.3 us -> 2.26 us
    unnamed x7 -> x1, local copies, waits for them, and re-layouts: 4.3 us -> 2.26 us
where the time goes in v2:
time: 61.6 us; the launch traced here: 61.4 us
  Pallas kernels  59.2 us (96%)
  local copies, waits for them, and re-layouts  2.26 us (4%)
    pallas_call x1, Pallas kernels, kernel_body(): pl.pallas_call(functools.partial(kernel, sizes), out_shape=jax.ShapeDtype...  59.2 us
    unnamed x1, local copies, waits for them, and re-layouts  2.26 us

profile of v2, /device:TPU:0, one launch (start us, length us, event | category | flops | bytes accessed | tf_op | source)
XLA Modules:
  0.0 61.4 jit_solution(8552917555569208889)
XLA Ops:
  0.0 59.2 %shard_map.46 = bf16[64,16,512]{2,1,0:T(8,128)(2,1)} custom-call(f32[3,512]{1,0:T(4,128)} %gain_hbm.1, bf16[1024,512]{1,0:T(8,128)(2,1)} %bitcast.5, bf16[3,512,1536]{2,1,0:T(8,128)(2,1)} %wi_hbm.1, bf16[3,512,512]{2,1,0:T(8,128)(2,1)} %wo_hbm.1), custom_call_target="tpu_custom_call" | custom-call | flops 6442450944 | bytes 4194304 | tf_op jit(solution)/shard_map/pallas_call | solution.py:310
  59.2 2.3 %copy.7 = bf16[64,1,16,512]{3,2,1,0:T(8,128)(2,1)} copy(bf16[64,1,16,512]{3,2,1,0:T(8,128)(2,1)} %bitcast.4) | data formatting | bytes 2097152

commit v3 on v2

--- a/solution.py
+++ b/solution.py
@@ -87,8 +87,8 @@
             s = s + bias
             e = jnp.exp(s - jnp.max(s, axis=-1, keepdims=True)).astype(jnp.bfloat16)
             o = jnp.dot(e, jnp.concatenate([v, ones], axis=1), preferred_element_type=jnp.float32)
-            o = o[:, :pair] / o[:, pair:]
-            heads.append(jnp.where(low, o[:GROUP], o[GROUP:]))
+            o = jnp.where(jnp.concatenate([low, low], axis=1), o[:GROUP], o[GROUP:])
+            heads.append(o[:, :pair] / o[:, pair:])
         groups.append(jnp.concatenate(heads, axis=1))
     mixed = jnp.concatenate(groups, axis=0).astype(jnp.bfloat16)
     return x + jnp.dot(mixed, w_out, preferred_element_type=jnp.float32)
@@ -131,25 +131,13 @@
         return {"aa": device // cores, "ba": device % cores}
 
     near = n // 2
-
-    def other(o):
-        side = me // near
-        side = jnp.where(o < near, 1 - side, side)
-        return side * near + lax.rem(me + o, near)
+    side = me // near
+    others = [(1 - side) * near + lax.rem(me + o, near) for o in range(near)]
+    others += [side * near + lax.rem(me + o, near) for o in range(1, near)]
 
     barrier = pltpu.get_barrier_semaphore()
-
-    def greet(o, c):
-        pl.semaphore_signal(barrier, inc=1, device_id=where(other(o)), device_id_type=MESH)
-        return c
-
-    def others(body):
-        def step(i, c):
-            return body(jnp.where(i < near, i, i + 1), c)
-
-        lax.fori_loop(0, n - 1, step, 0)
-
-    others(greet)
+    for device in others:
+        pl.semaphore_signal(barrier, inc=1, device_id=where(device), device_id_type=MESH)
     for copy in x_copies:
         copy.wait()
     for p in range(planes):
@@ -162,28 +150,29 @@
 
     spots = [(w, f) for w in range(wide) for f in range(mine)]
 
-    def along_frames(k):
+    def along_frames(ks):
         x = jnp.concatenate(
-            [load_strided(x32, f * cols + k * wide + w, n, mine * cols) for w, f in spots], axis=0
+            [
+                load_strided(x32, f * cols + k * wide + w, n, mine * cols)
+                for k in ks
+                for w, f in spots
+            ],
+            axis=0,
         )
         return block_on(x, gain_ref[0:1, :], wi_ref[0], wo_ref[0], lambda i: i // frames)
 
     def give_chunk(k):
         recv[k, ba, aa] = send[k, me]
 
-        def give(o, c):
-            device = other(o)
+        for device in others:
             pltpu.make_async_remote_copy(
                 src_ref=send.at[k, device], dst_ref=recv.at[k, ba, aa],
                 send_sem=send_sem, recv_sem=recv_sem.at[k],
                 device_id=where(device), device_id_type=MESH,
             ).start()
-            return c
-
-        others(give)
 
     def first(k, c):
-        y = along_frames(k)
+        y = along_frames([k])
         for at, (w, f) in enumerate(spots):
             for p in range(planes):
                 turned[p, pl.ds(w * mine + f, n, stride=PIECE), :] = y[
@@ -198,17 +187,13 @@
 
     lax.fori_loop(0, early, first, 0)
 
-    def first_late(k, c):
-        y = along_frames(early + k)
-        for at, (w, f) in enumerate(spots):
-            row = (f // few) * n * PIECE + (k * wide + w) * few + f % few
-            for p in range(planes):
-                late[p, pl.ds(row, n, stride=PIECE), :] = y[
-                    at * n : (at + 1) * n, p * LANES : (p + 1) * LANES
-                ]
-        return c
-
-    lax.fori_loop(0, early, first_late, 0)
+    y = along_frames(range(early, 2 * early))
+    for at, (k, w, f) in enumerate((k, w, f) for k in range(early) for w, f in spots):
+        row = (f // few) * n * PIECE + (k * wide + w) * few + f % few
+        for p in range(planes):
+            late[p, pl.ds(row, n, stride=PIECE), :] = y[
+                at * n : (at + 1) * n, p * LANES : (p + 1) * LANES
+            ]
     for h in range(mine // few):
         for p in range(planes):
             send[early + h, :, :, p * LANES : (p + 1) * LANES] = (
@@ -221,22 +206,24 @@
     for copy in w_copies[2:]:
         copy.wait()
 
-    def along_rows(k):
+    def arrived(k):
         pltpu.make_async_copy(send.at[0, 0 : n - 1], send.at[0, 0 : n - 1], recv_sem.at[k]).wait()
-        x = recv[k].reshape(n * PIECE, d).astype(jnp.float32)
+
+    def along_rows(chunks):
+        x = chunks.reshape(-1, d).astype(jnp.float32)
         return block_on(x, gain_ref[1:2, :], wi_ref[1], wo_ref[1], lambda i: i % PIECE)
 
-    def second(k, c):
-        y = along_rows(k)
+    for k in range(early):
+        arrived(k)
+    y = along_rows(recv[0:early])
+    for k in range(early):
         for at in range(n):
-            place = pl.multiple_of((at * early + k) * PIECE, PIECE)
+            place = (at * early + k) * PIECE
+            come = (k * n + at) * PIECE
             for p in range(planes):
-                y1[p, pl.ds(place, PIECE), :] = y[
-                    at * PIECE : (at + 1) * PIECE, p * LANES : (p + 1) * LANES
+                y1[p, place : place + PIECE, :] = y[
+                    come : come + PIECE, p * LANES : (p + 1) * LANES
                 ]
-        return c
-
-    lax.fori_loop(0, early, second, 0)
 
     some = GROUP // (cores * cols)
 
@@ -265,19 +252,16 @@
             back.at[f, place(me)], out_ref.at[frame], own_sem.at[f]
         ).start()
 
-        def give(o, c):
-            device = other(o)
+        for device in others:
             pltpu.make_async_remote_copy(
                 src_ref=back.at[f, place(device)], dst_ref=out_ref.at[frame],
                 send_sem=back_sem, recv_sem=out_sem,
                 device_id=where(device), device_id_type=MESH,
             ).start()
-            return c
-
-        others(give)
 
     def rest(h, c):
-        y = along_rows(early + h)
+        arrived(early + h)
+        y = along_rows(recv[early + h])
         for p in range(planes):
             y1_late[p] = y[:, p * LANES : (p + 1) * LANES]
 
@@ -334,7 +318,7 @@
             dma((mine,)),
         ],
         compiler_params=pltpu.CompilerParams(
-            collective_id=0, has_side_effects=True, vmem_limit_bytes=62 * 1024 * 1024
+            collective_id=0, has_side_effects=True, vmem_limit_bytes=52 * 1024 * 1024
         ),
         cost_estimate=pl.CostEstimate(
             flops=2 * tokens * d * 4 * d * 3, bytes_accessed=8 * tokens * d, transcendentals=0

time: 61.6 us -> 60.9 us (0.989)
    unnamed x1 -> x3, local copies, waits for them, and re-layouts: 2.26 us -> 1.67 us
where the time goes in v3:
time: 60.9 us; the launch traced here: 60.7 us
  Pallas kernels  59.1 us (97%)
  local copies, waits for them, and re-layouts  1.67 us (3%)
    pallas_call x1, Pallas kernels, kernel_body(): pl.pallas_call(functools.partial(kernel, sizes), out_shape=jax.ShapeDtype...  59.1 us
    unnamed x3, local copies, waits for them, and re-layouts  1.67 us

profile of v3, /device:TPU:0, one launch (start us, length us, event | category | flops | bytes accessed | tf_op | source)
XLA Modules:
  0.0 60.7 jit_solution(7815163765527032821)
XLA Ops:
  0.0 0.0 copy-start
  0.0 0.7 %copy-done = f32[3,512]{1,0:T(4,128)S(1)} copy-done((f32[3,512]{1,0:T(4,128)S(1)}, f32[3,512]{1,0:T(4,128)}, u32[]{:S(2)}) %copy-start) | copy-done | bytes 6168
  0.7 59.1 %shard_map.46 = bf16[64,16,512]{2,1,0:T(8,128)(2,1)S(1)} custom-call(f32[3,512]{1,0:T(4,128)S(1)} %copy-done, bf16[1024,512]{1,0:T(8,128)(2,1)} %bitcast.5, bf16[3,512,1536]{2,1,0:T(8,128)(2,1)} %wi_hbm.1, bf16[3,512,512]{2,1,0:T(8,128)(2,1)} %wo_hbm.1), custom_call_target="tpu_custom_call" | custom-call | flops 6442450944 | bytes 4194304 | tf_op jit(solution)/shard_map/pallas_call | solution.py:294
  59.8 1.0 %copy.7 = bf16[64,1,16,512]{3,2,1,0:T(8,128)(2,1)} copy(bf16[64,1,16,512]{3,2,1,0:T(8,128)(2,1)S(1)} %bitcast.4) | data formatting | bytes 2097152
Async XLA Ops:
  0.0 0.7 %copy-start = (f32[3,512]{1,0:T(4,128)S(1)}, f32[3,512]{1,0:T(4,128)}, u32[]{:S(2)}) copy-start(f32[3,512]{1,0:T(4,128)} %gain_hbm.1) | copy-start | bytes 18436

commit v4 on v3

--- a/solution.py
+++ b/solution.py
@@ -132,8 +132,11 @@
 
     near = n // 2
     side = me // near
-    others = [(1 - side) * near + lax.rem(me + o, near) for o in range(near)]
-    others += [side * near + lax.rem(me + o, near) for o in range(1, near)]
+    others = []
+    for o in range(near):
+        if o:
+            others.append(side * near + lax.rem(me + o, near))
+        others.append((1 - side) * near + lax.rem(me + o, near))
 
     barrier = pltpu.get_barrier_semaphore()
     for device in others:

time: 60.9 us -> 61.4 us (level)
  no operation moved by 1% of the time
where the time goes in v4:
time: 61.4 us; the launch traced here: 61.2 us
  Pallas kernels  59.5 us (97%)
  local copies, waits for them, and re-layouts  1.67 us (3%)
    pallas_call x1, Pallas kernels, kernel_body(): pl.pallas_call(functools.partial(kernel, sizes), out_shape=jax.ShapeDtype...  59.5 us
    unnamed x3, local copies, waits for them, and re-layouts  1.67 us

profile of v4, /device:TPU:0, one launch (start us, length us, event | category | flops | bytes accessed | tf_op | source)
XLA Modules:
  0.0 61.2 jit_solution(17267745683406097355)
XLA Ops:
  0.0 0.0 copy-start
  0.0 0.7 %copy-done = f32[3,512]{1,0:T(4,128)S(1)} copy-done((f32[3,512]{1,0:T(4,128)S(1)}, f32[3,512]{1,0:T(4,128)}, u32[]{:S(2)}) %copy-start) | copy-done | bytes 6168
  0.7 59.5 %shard_map.46 = bf16[64,16,512]{2,1,0:T(8,128)(2,1)S(1)} custom-call(f32[3,512]{1,0:T(4,128)S(1)} %copy-done, bf16[1024,512]{1,0:T(8,128)(2,1)} %bitcast.5, bf16[3,512,1536]{2,1,0:T(8,128)(2,1)} %wi_hbm.1, bf16[3,512,512]{2,1,0:T(8,128)(2,1)} %wo_hbm.1), custom_call_target="tpu_custom_call" | custom-call | flops 6442450944 | bytes 4194304 | tf_op jit(solution)/shard_map/pallas_call | solution.py:297
  60.2 1.0 %copy.7 = bf16[64,1,16,512]{3,2,1,0:T(8,128)(2,1)} copy(bf16[64,1,16,512]{3,2,1,0:T(8,128)(2,1)S(1)} %bitcast.4) | data formatting | bytes 2097152
Async XLA Ops:
  0.0 0.7 %copy-start = (f32[3,512]{1,0:T(4,128)S(1)}, f32[3,512]{1,0:T(4,128)}, u32[]{:S(2)}) copy-start(f32[3,512]{1,0:T(4,128)} %gain_hbm.1) | copy-start | bytes 18436

commit v5 on v3

--- a/solution.py
+++ b/solution.py
@@ -57,21 +57,24 @@
     return lax.all_to_all(state, "aa", split_axis=1, concat_axis=0, tiled=True)
 
 
-def block_on(x, gain, w_in, w_out, line_of):
+def mask_of(line_of):
+    rows = line_of(lax.broadcasted_iota(jnp.int32, (2 * GROUP, GROUP), 0) % GROUP)
+    cols = line_of(lax.broadcasted_iota(jnp.int32, (2 * GROUP, GROUP), 1))
+    return jnp.where(rows == cols, 0.0, -jnp.inf)
+
+
+def block_on(x, gain, w_in, w_out, bias_ref):
     tokens, d = x.shape
     meansq = jnp.mean(x * x, axis=-1, keepdims=True)
     normed = (x * lax.rsqrt(meansq + 1e-06) * gain).astype(jnp.bfloat16)
-    packed = jnp.dot(normed, w_in, preferred_element_type=jnp.float32)
+    packed = jnp.dot(normed, w_in, preferred_element_type=jnp.float32).astype(jnp.bfloat16)
 
     pair = 2 * HEAD_DIM
     lane = lax.broadcasted_iota(jnp.int32, (GROUP, pair), 1)
     low = lane < HEAD_DIM
     scale = 1.0 / math.sqrt(HEAD_DIM)
-    keep_low = jnp.where(low, scale, 0.0)
-    keep_high = jnp.where(low, 0.0, scale)
-    rows = line_of(lax.broadcasted_iota(jnp.int32, (2 * GROUP, GROUP), 0) % GROUP)
-    cols = line_of(lax.broadcasted_iota(jnp.int32, (2 * GROUP, GROUP), 1))
-    bias = jnp.where(rows == cols, 0.0, -jnp.inf)
+    keep_low = jnp.where(low, scale, 0.0).astype(jnp.bfloat16)
+    keep_high = jnp.where(low, 0.0, scale).astype(jnp.bfloat16)
     ones = jnp.ones((GROUP, pair), jnp.bfloat16)
 
     groups = []
@@ -80,15 +83,18 @@
         heads = []
         for p in range(d // pair):
             q = packed[at, p * pair : (p + 1) * pair]
-            k = packed[at, d + p * pair : d + (p + 1) * pair].astype(jnp.bfloat16)
-            v = packed[at, 2 * d + p * pair : 2 * d + (p + 1) * pair].astype(jnp.bfloat16)
-            q2 = jnp.concatenate([q * keep_low, q * keep_high], axis=0).astype(jnp.bfloat16)
+            k = packed[at, d + p * pair : d + (p + 1) * pair]
+            v = packed[at, 2 * d + p * pair : 2 * d + (p + 1) * pair]
+            q2 = jnp.concatenate([q * keep_low, q * keep_high], axis=0)
             s = lax.dot_general(q2, k, (((1,), (1,)), ((), ())), preferred_element_type=jnp.float32)
-            s = s + bias
+            s = s + bias_ref[...]
             e = jnp.exp(s - jnp.max(s, axis=-1, keepdims=True)).astype(jnp.bfloat16)
             o = jnp.dot(e, jnp.concatenate([v, ones], axis=1), preferred_element_type=jnp.float32)
             o = jnp.where(jnp.concatenate([low, low], axis=1), o[:GROUP], o[GROUP:])
-            heads.append(o[:, :pair] / o[:, pair:])
+            total = o[:, pair:]
+            inverse = pl.reciprocal(total, approx=True)
+            inverse = inverse * (2.0 - total * inverse)
+            heads.append(o[:, :pair] * inverse)
         groups.append(jnp.concatenate(heads, axis=1))
     mixed = jnp.concatenate(groups, axis=0).astype(jnp.bfloat16)
     return x + jnp.dot(mixed, w_out, preferred_element_type=jnp.float32)
@@ -102,7 +108,7 @@
 
 def kernel(
     sizes, gain_hbm, x_hbm, wi_hbm, wo_hbm, out_ref,
-    gain_ref, x_ref, wi_ref, wo_ref, x32, turned, late, send, recv, y1, y1_late, back,
+    bias_ref, gain_ref, x_ref, wi_ref, wo_ref, x32, turned, late, send, recv, y1, y1_late, back,
     x_sem, w_sem, send_sem, recv_sem, back_sem, out_sem, own_sem,
 ):
     frames, rows, cols, n, cores = sizes
@@ -111,6 +117,7 @@
     half = cols // 2
     early = half // wide
     few = PIECE // half
+    some = GROUP // (cores * cols)
     d = x_ref.shape[-1]
     planes = d // LANES
     aa, ba = lax.axis_index("aa"), lax.axis_index("ba")
@@ -138,6 +145,9 @@
     barrier = pltpu.get_barrier_semaphore()
     for device in others:
         pl.semaphore_signal(barrier, inc=1, device_id=where(device), device_id_type=MESH)
+    bias_ref[0] = mask_of(lambda i: i // frames)
+    bias_ref[1] = mask_of(lambda i: i % PIECE)
+    bias_ref[2] = mask_of(lambda i: (i // half) % some)
     for copy in x_copies:
         copy.wait()
     for p in range(planes):
@@ -159,7 +169,7 @@
             ],
             axis=0,
         )
-        return block_on(x, gain_ref[0:1, :], wi_ref[0], wo_ref[0], lambda i: i // frames)
+        return block_on(x, gain_ref[0:1, :], wi_ref[0], wo_ref[0], bias_ref.at[0])
 
     def give_chunk(k):
         recv[k, ba, aa] = send[k, me]
@@ -211,7 +221,7 @@
 
     def along_rows(chunks):
         x = chunks.reshape(-1, d).astype(jnp.float32)
-        return block_on(x, gain_ref[1:2, :], wi_ref[1], wo_ref[1], lambda i: i % PIECE)
+        return block_on(x, gain_ref[1:2, :], wi_ref[1], wo_ref[1], bias_ref.at[1])
 
     for k in range(early):
         arrived(k)
@@ -225,7 +235,6 @@
                     come : come + PIECE, p * LANES : (p + 1) * LANES
                 ]
 
-    some = GROUP // (cores * cols)
 
     def third(h, i):
         f = h * few + i
@@ -236,7 +245,7 @@
                 parts.append(load_strided(y1, at * half * mine + f, some * half, mine))
                 parts.append(load_strided(y1_late, at * half * few + i, some * half, few))
         x = jnp.concatenate(parts, axis=0)
-        y = block_on(x, gain_ref[2:3, :], wi_ref[2], wo_ref[2], lambda t: (t // half) % some)
+        y = block_on(x, gain_ref[2:3, :], wi_ref[2], wo_ref[2], bias_ref.at[2])
         for at in range(n):
             low = (at // some) * 2 * some * half + (at % some) * half
             high = low + some * half
@@ -297,6 +306,7 @@
         in_specs=[pl.BlockSpec(memory_space=pltpu.HBM)] * 4,
         out_specs=pl.BlockSpec(memory_space=pl.ANY),
         scratch_shapes=[
+            pltpu.VMEM((3, 2 * GROUP, GROUP), jnp.float32),
             pltpu.VMEM(norm_gain.shape, jnp.float32),
             pltpu.VMEM((tokens, d), jnp.bfloat16),
             pltpu.VMEM(qkv_weight.shape, jnp.bfloat16),

time: 60.9 us -> 60.9 us (level)
  no operation moved by 1% of the time
where the time goes in v5:
time: 60.9 us; the launch traced here: 60.7 us
  Pallas kernels  59 us (97%)
  local copies, waits for them, and re-layouts  1.67 us (3%)
    pallas_call x1, Pallas kernels, kernel_body(): pl.pallas_call(functools.partial(kernel, sizes), out_shape=jax.ShapeDtype...  59 us
    unnamed x3, local copies, waits for them, and re-layouts  1.67 us

profile of v5, /device:TPU:0, one launch (start us, length us, event | category | flops | bytes accessed | tf_op | source)
XLA Modules:
  0.0 60.7 jit_solution(4943977748819804549)
XLA Ops:
  0.0 0.0 copy-start
  0.0 0.7 %copy-done = f32[3,512]{1,0:T(4,128)S(1)} copy-done((f32[3,512]{1,0:T(4,128)S(1)}, f32[3,512]{1,0:T(4,128)}, u32[]{:S(2)}) %copy-start) | copy-done | bytes 6168
  0.7 59.0 %shard_map.46 = bf16[64,16,512]{2,1,0:T(8,128)(2,1)S(1)} custom-call(f32[3,512]{1,0:T(4,128)S(1)} %copy-done, bf16[1024,512]{1,0:T(8,128)(2,1)} %bitcast.5, bf16[3,512,1536]{2,1,0:T(8,128)(2,1)} %wi_hbm.1, bf16[3,512,512]{2,1,0:T(8,128)(2,1)} %wo_hbm.1), custom_call_target="tpu_custom_call" | custom-call | flops 6442450944 | bytes 4194304 | tf_op jit(solution)/shard_map/pallas_call | solution.py:303
  59.7 1.0 %copy.7 = bf16[64,1,16,512]{3,2,1,0:T(8,128)(2,1)} copy(bf16[64,1,16,512]{3,2,1,0:T(8,128)(2,1)S(1)} %bitcast.4) | data formatting | bytes 2097152
Async XLA Ops:
  0.0 0.7 %copy-start = (f32[3,512]{1,0:T(4,128)S(1)}, f32[3,512]{1,0:T(4,128)}, u32[]{:S(2)}) copy-start(f32[3,512]{1,0:T(4,128)} %gain_hbm.1) | copy-start | bytes 18436

commit v6 on v5

--- a/solution.py
+++ b/solution.py
@@ -63,11 +63,11 @@
     return jnp.where(rows == cols, 0.0, -jnp.inf)
 
 
-def block_on(x, gain, w_in, w_out, bias_ref):
+def block_on(x, gain, w_in_ref, w_out_ref, masks, before_out=None):
     tokens, d = x.shape
     meansq = jnp.mean(x * x, axis=-1, keepdims=True)
     normed = (x * lax.rsqrt(meansq + 1e-06) * gain).astype(jnp.bfloat16)
-    packed = jnp.dot(normed, w_in, preferred_element_type=jnp.float32).astype(jnp.bfloat16)
+    packed = jnp.dot(normed, w_in_ref[...], preferred_element_type=jnp.float32).astype(jnp.bfloat16)
 
     pair = 2 * HEAD_DIM
     lane = lax.broadcasted_iota(jnp.int32, (GROUP, pair), 1)
@@ -87,7 +87,7 @@
             v = packed[at, 2 * d + p * pair : 2 * d + (p + 1) * pair]
             q2 = jnp.concatenate([q * keep_low, q * keep_high], axis=0)
             s = lax.dot_general(q2, k, (((1,), (1,)), ((), ())), preferred_element_type=jnp.float32)
-            s = s + bias_ref[...]
+            s = s + masks[g][...]
             e = jnp.exp(s - jnp.max(s, axis=-1, keepdims=True)).astype(jnp.bfloat16)
             o = jnp.dot(e, jnp.concatenate([v, ones], axis=1), preferred_element_type=jnp.float32)
             o = jnp.where(jnp.concatenate([low, low], axis=1), o[:GROUP], o[GROUP:])
@@ -97,7 +97,9 @@
             heads.append(o[:, :pair] * inverse)
         groups.append(jnp.concatenate(heads, axis=1))
     mixed = jnp.concatenate(groups, axis=0).astype(jnp.bfloat16)
-    return x + jnp.dot(mixed, w_out, preferred_element_type=jnp.float32)
+    if before_out is not None:
+        before_out()
+    return x + jnp.dot(mixed, w_out_ref[...], preferred_element_type=jnp.float32)
 
 
 def load_strided(ref, start, size, stride):
@@ -108,8 +110,8 @@
 
 def kernel(
     sizes, gain_hbm, x_hbm, wi_hbm, wo_hbm, out_ref,
-    bias_ref, gain_ref, x_ref, wi_ref, wo_ref, x32, turned, late, send, recv, y1, y1_late, back,
-    x_sem, w_sem, send_sem, recv_sem, back_sem, out_sem, own_sem,
+    bias_ref, gain_ref, x_ref, wi_ref, wo_ref, x32, turned, late, send_short, recv_short, send, recv, y1, y1_late, back,
+    x_sem, w_sem, short_sem, send_sem, recv_sem, back_sem, out_sem, own_sem,
 ):
     frames, rows, cols, n, cores = sizes
     mine = frames // n
@@ -120,6 +122,7 @@
     some = GROUP // (cores * cols)
     d = x_ref.shape[-1]
     planes = d // LANES
+    short = PIECE // 2
     aa, ba = lax.axis_index("aa"), lax.axis_index("ba")
     me = aa * cores + ba
 
@@ -148,19 +151,16 @@
     bias_ref[0] = mask_of(lambda i: i // frames)
     bias_ref[1] = mask_of(lambda i: i % PIECE)
     bias_ref[2] = mask_of(lambda i: (i // half) % some)
+    bias_ref[3] = mask_of(lambda i: i // (rows * short) * short + i % short)
     for copy in x_copies:
         copy.wait()
     for p in range(planes):
         x32[p] = x_ref[:, p * LANES : (p + 1) * LANES].astype(jnp.float32)
-    for copy in w_copies[:2]:
-        copy.wait()
-    for copy in w_copies[2:]:
-        copy.start()
-    pl.semaphore_wait(barrier, n - 1)
+    w_copies[0].wait()
 
     spots = [(w, f) for w in range(wide) for f in range(mine)]
 
-    def along_frames(ks):
+    def along_frames(ks, spots, before_out=None):
         x = jnp.concatenate(
             [
                 load_strided(x32, f * cols + k * wide + w, n, mine * cols)
@@ -169,7 +169,8 @@
             ],
             axis=0,
         )
-        return block_on(x, gain_ref[0:1, :], wi_ref[0], wo_ref[0], bias_ref.at[0])
+        masks = [bias_ref.at[0]] * (x.shape[0] // GROUP)
+        return block_on(x, gain_ref[0:1, :], wi_ref.at[0], wo_ref.at[0], masks, before_out)
 
     def give_chunk(k):
         recv[k, ba, aa] = send[k, me]
@@ -181,8 +182,36 @@
                 device_id=where(device), device_id_type=MESH,
             ).start()
 
-    def first(k, c):
-        y = along_frames([k])
+    def more_weights():
+        w_copies[1].wait()
+        for copy in w_copies[2:]:
+            copy.start()
+
+    for part in range(2):
+        these = spots[part * short : (part + 1) * short]
+        y = along_frames([0], these, None if part else more_weights)
+        for at in range(short):
+            for p in range(planes):
+                row = p // (planes // 2) * short + at
+                turned[p % (planes // 2), pl.ds(row, n, stride=PIECE), :] = y[
+                    at * n : (at + 1) * n, p * LANES : (p + 1) * LANES
+                ]
+        for p in range(planes // 2):
+            send_short[part, :, :, p * LANES : (p + 1) * LANES] = (
+                turned[p].astype(jnp.bfloat16).reshape(n, PIECE, LANES)
+            )
+        recv_short[part, ba, aa] = send_short[part, me]
+        if part == 0:
+            pl.semaphore_wait(barrier, n - 1)
+        for device in others:
+            pltpu.make_async_remote_copy(
+                src_ref=send_short.at[part, device], dst_ref=recv_short.at[part, ba, aa],
+                send_sem=short_sem.at[2], recv_sem=short_sem.at[part],
+                device_id=where(device), device_id_type=MESH,
+            ).start()
+
+    for k in range(1, early):
+        y = along_frames([k], spots)
         for at, (w, f) in enumerate(spots):
             for p in range(planes):
                 turned[p, pl.ds(w * mine + f, n, stride=PIECE), :] = y[
@@ -193,11 +222,8 @@
                 turned[p].astype(jnp.bfloat16).reshape(n, PIECE, LANES)
             )
         give_chunk(k)
-        return c
-
-    lax.fori_loop(0, early, first, 0)
-
-    y = along_frames(range(early, 2 * early))
+
+    y = along_frames(range(early, 2 * early), spots)
     for at, (k, w, f) in enumerate((k, w, f) for k in range(early) for w, f in spots):
         row = (f // few) * n * PIECE + (k * wide + w) * few + f % few
         for p in range(planes):
@@ -219,21 +245,34 @@
     def arrived(k):
         pltpu.make_async_copy(send.at[0, 0 : n - 1], send.at[0, 0 : n - 1], recv_sem.at[k]).wait()
 
-    def along_rows(chunks):
-        x = chunks.reshape(-1, d).astype(jnp.float32)
-        return block_on(x, gain_ref[1:2, :], wi_ref[1], wo_ref[1], bias_ref.at[1])
-
-    for k in range(early):
+    def along_rows(x, masks):
+        return block_on(x, gain_ref[1:2, :], wi_ref.at[1], wo_ref.at[1], masks)
+
+    parts = []
+    for part in range(2):
+        all_short = send_short.at[0, 0 : n - 1]
+        pltpu.make_async_copy(all_short, all_short, short_sem.at[part]).wait()
+        x = recv_short[part].reshape(n, PIECE, d // 2).astype(jnp.float32)
+        x = jnp.concatenate([x[:, :short], x[:, short:]], axis=-1)
+        parts.append(x.reshape(n * short, d))
+    for k in range(1, early):
         arrived(k)
-    y = along_rows(recv[0:early])
-    for k in range(early):
-        for at in range(n):
-            place = (at * early + k) * PIECE
-            come = (k * n + at) * PIECE
-            for p in range(planes):
-                y1[p, place : place + PIECE, :] = y[
-                    come : come + PIECE, p * LANES : (p + 1) * LANES
-                ]
+        parts.append(recv[k].reshape(n * PIECE, d).astype(jnp.float32))
+    x = jnp.concatenate(parts, axis=0)
+    y = along_rows(x, [bias_ref.at[3]] * 2 + [bias_ref.at[1]] * (x.shape[0] // GROUP - 2))
+    moves = [
+        (at * early * PIECE + part * short, (part * n + at) * short, short)
+        for part in range(2)
+        for at in range(n)
+    ]
+    moves += [
+        ((at * early + k) * PIECE, (k * n + at) * PIECE, PIECE)
+        for k in range(1, early)
+        for at in range(n)
+    ]
+    for place, come, size in moves:
+        for p in range(planes):
+            y1[p, place : place + size, :] = y[come : come + size, p * LANES : (p + 1) * LANES]
 
 
     def third(h, i):
@@ -245,7 +284,8 @@
                 parts.append(load_strided(y1, at * half * mine + f, some * half, mine))
                 parts.append(load_strided(y1_late, at * half * few + i, some * half, few))
         x = jnp.concatenate(parts, axis=0)
-        y = block_on(x, gain_ref[2:3, :], wi_ref[2], wo_ref[2], bias_ref.at[2])
+        masks = [bias_ref.at[2]] * (rows // some)
+        y = block_on(x, gain_ref[2:3, :], wi_ref.at[2], wo_ref.at[2], masks)
         for at in range(n):
             low = (at // some) * 2 * some * half + (at % some) * half
             high = low + some * half
@@ -270,7 +310,8 @@
 
     def rest(h, c):
         arrived(early + h)
-        y = along_rows(recv[early + h])
+        x = recv[early + h].reshape(n * PIECE, d).astype(jnp.float32)
+        y = along_rows(x, [bias_ref.at[1]] * (x.shape[0] // GROUP))
         for p in range(planes):
             y1_late[p] = y[:, p * LANES : (p + 1) * LANES]
 
@@ -284,7 +325,7 @@
 
     for f in range(mine):
         pltpu.make_async_copy(back.at[f, 0], out_ref.at[f], own_sem.at[f]).wait()
-    for sem, buffer in ((send_sem, send), (back_sem, back)):
+    for sem, buffer in ((short_sem.at[2], send_short), (send_sem, send.at[1:]), (back_sem, back)):
         pltpu.make_async_copy(
             buffer.at[:, 0 : n - 1], buffer.at[:, 0 : n - 1], sem
         ).wait()
@@ -306,7 +347,7 @@
         in_specs=[pl.BlockSpec(memory_space=pltpu.HBM)] * 4,
         out_specs=pl.BlockSpec(memory_space=pl.ANY),
         scratch_shapes=[
-            pltpu.VMEM((3, 2 * GROUP, GROUP), jnp.float32),
+            pltpu.VMEM((4, 2 * GROUP, GROUP), jnp.float32),
             pltpu.VMEM(norm_gain.shape, jnp.float32),
             pltpu.VMEM((tokens, d), jnp.bfloat16),
             pltpu.VMEM(qkv_weight.shape, jnp.bfloat16),
@@ -314,6 +355,8 @@
             pltpu.VMEM((planes, tokens, LANES), jnp.float32),
             pltpu.VMEM((planes, n * PIECE, LANES), jnp.float32),
             pltpu.VMEM((planes, tokens // 2, LANES), jnp.float32),
+            pltpu.VMEM((2, n, PIECE, d // 2), jnp.bfloat16),
+            pltpu.VMEM((2, cores, n // cores, PIECE, d // 2), jnp.bfloat16),
             pltpu.VMEM((chunks, n, PIECE, d), jnp.bfloat16),
             pltpu.VMEM((chunks, cores, n // cores, PIECE, d), jnp.bfloat16),
             pltpu.VMEM((planes, tokens // 2, LANES), jnp.float32),
@@ -321,6 +364,7 @@
             pltpu.VMEM((mine, n, cols, d), jnp.bfloat16),
             dma((2,)),
             dma((3, 2)),
+            dma((3,)),
             dma,
             dma((chunks,)),
             dma,
@@ -346,6 +390,8 @@
     half = cols // 2
     if half % (PIECE // mine) or mine % (PIECE // half):
         return False
+    if PIECE // mine % 2 or n * PIECE != 2 * GROUP or d % (2 * LANES):
+        return False
     return GROUP % (cores * cols) == 0 and (n * PIECE) % GROUP == 0
 
 

time: 60.9 us -> 58.2 us (0.956)
  Pallas kernels: 59 us -> 56.4 us
    pallas_call x1, Pallas kernels: 59 us -> 56.4 us  [kernel_body(): pl.pallas_call(functools.partial(kernel, sizes), out_shape=jax.ShapeDtype...]
where the time goes in v6:
time: 58.2 us; the launch traced here: 58 us
  Pallas kernels  56.4 us (97%)
  local copies, waits for them, and re-layouts  1.67 us (3%)
    pallas_call x1, Pallas kernels, kernel_body(): pl.pallas_call(functools.partial(kernel, sizes), out_shape=jax.ShapeDtype...  56.4 us
    unnamed x3, local copies, waits for them, and re-layouts  1.67 us

profile of v6, /device:TPU:0, one launch (start us, length us, event | category | flops | bytes accessed | tf_op | source)
XLA Modules:
  0.0 58.0 jit_solution(9967118573490172265)
XLA Ops:
  0.0 0.0 copy-start
  0.0 0.7 %copy-done = f32[3,512]{1,0:T(4,128)S(1)} copy-done((f32[3,512]{1,0:T(4,128)S(1)}, f32[3,512]{1,0:T(4,128)}, u32[]{:S(2)}) %copy-start) | copy-done | bytes 6168
  0.7 56.4 %shard_map.46 = bf16[64,16,512]{2,1,0:T(8,128)(2,1)S(1)} custom-call(f32[3,512]{1,0:T(4,128)S(1)} %copy-done, bf16[1024,512]{1,0:T(8,128)(2,1)} %bitcast.5, bf16[3,512,1536]{2,1,0:T(8,128)(2,1)} %wi_hbm.1, bf16[3,512,512]{2,1,0:T(8,128)(2,1)} %wo_hbm.1), custom_call_target="tpu_custom_call" | custom-call | flops 6442450944 | bytes 4194304 | tf_op jit(solution)/shard_map/pallas_call | solution.py:344
  57.1 1.0 %copy.7 = bf16[64,1,16,512]{3,2,1,0:T(8,128)(2,1)} copy(bf16[64,1,16,512]{3,2,1,0:T(8,128)(2,1)S(1)} %bitcast.4) | data formatting | bytes 2097152
Async XLA Ops:
  0.0 0.7 %copy-start = (f32[3,512]{1,0:T(4,128)S(1)}, f32[3,512]{1,0:T(4,128)}, u32[]{:S(2)}) copy-start(f32[3,512]{1,0:T(4,128)} %gain_hbm.1) | copy-start | bytes 18436

commit v7 on v6

--- a/solution.py
+++ b/solution.py
@@ -277,36 +277,32 @@
 
     def third(h, i):
         f = h * few + i
-        parts = []
-        for r in range(0, rows, some):
+        frame = me * mine + f
+        for g, part in enumerate((1 - side, side)):
+            parts = []
             for b in range(cores):
-                at = b * rows + r
+                at = b * rows + part * some
                 parts.append(load_strided(y1, at * half * mine + f, some * half, mine))
                 parts.append(load_strided(y1_late, at * half * few + i, some * half, few))
-        x = jnp.concatenate(parts, axis=0)
-        masks = [bias_ref.at[2]] * (rows // some)
-        y = block_on(x, gain_ref[2:3, :], wi_ref.at[2], wo_ref.at[2], masks)
-        for at in range(n):
-            low = (at // some) * 2 * some * half + (at % some) * half
-            high = low + some * half
-            piece = jnp.concatenate([y[low : low + half], y[high : high + half]], axis=0)
-            back[f, at] = piece.astype(jnp.bfloat16)
-        frame = me * mine + f
-
-        def place(device):
-            r, b = device // cores, device % cores
-            return ((r // some) * cores + b) * some + r % some
-
-        pltpu.make_async_copy(
-            back.at[f, place(me)], out_ref.at[frame], own_sem.at[f]
-        ).start()
-
-        for device in others:
-            pltpu.make_async_remote_copy(
-                src_ref=back.at[f, place(device)], dst_ref=out_ref.at[frame],
-                send_sem=back_sem, recv_sem=out_sem,
-                device_id=where(device), device_id_type=MESH,
-            ).start()
+            x = jnp.concatenate(parts, axis=0)
+            y = block_on(x, gain_ref[2:3, :], wi_ref.at[2], wo_ref.at[2], [bias_ref.at[2]])
+            for b in range(cores):
+                for r in range(some):
+                    low = (b * 2 * some + r) * half
+                    high = low + some * half
+                    piece = jnp.concatenate([y[low : low + half], y[high : high + half]], axis=0)
+                    back[f, g * near + r * cores + b] = piece.astype(jnp.bfloat16)
+            if g:
+                pltpu.make_async_copy(
+                    back.at[f, near + lax.rem(me, near)], out_ref.at[frame], own_sem.at[f]
+                ).start()
+            for o in range(g, near):
+                turn = lax.rem(me + o, near)
+                pltpu.make_async_remote_copy(
+                    src_ref=back.at[f, g * near + turn], dst_ref=out_ref.at[frame],
+                    send_sem=back_sem, recv_sem=out_sem,
+                    device_id=where(part * near + turn), device_id_type=MESH,
+                ).start()
 
     def rest(h, c):
         arrived(early + h)
@@ -390,7 +386,7 @@
     half = cols // 2
     if half % (PIECE // mine) or mine % (PIECE // half):
         return False
-    if PIECE // mine % 2 or n * PIECE != 2 * GROUP or d % (2 * LANES):
+    if PIECE // mine % 2 or n * PIECE != 2 * GROUP or rows * cores * cols != 2 * GROUP or d % (2 * LANES):
         return False
     return GROUP % (cores * cols) == 0 and (n * PIECE) % GROUP == 0
 

time: 58.2 us -> 57.5 us (0.988)
  Pallas kernels: 56.4 us -> 55.6 us
    pallas_call x1, Pallas kernels: 56.4 us -> 55.6 us  [kernel_body(): pl.pallas_call(functools.partial(kernel, sizes), out_shape=jax.ShapeDtype...]
where the time goes in v7:
time: 57.5 us; the launch traced here: 57.3 us
  Pallas kernels  55.6 us (97%)
  local copies, waits for them, and re-layouts  1.67 us (3%)
    pallas_call x1, Pallas kernels, kernel_body(): pl.pallas_call(functools.partial(kernel, sizes), out_shape=jax.ShapeDtype...  55.6 us
    unnamed x3, local copies, waits for them, and re-layouts  1.67 us

profile of v7, /device:TPU:0, one launch (start us, length us, event | category | flops | bytes accessed | tf_op | source)
XLA Modules:
  0.0 57.3 jit_solution(165821103214931577)
XLA Ops:
  0.0 0.0 copy-start
  0.0 0.7 %copy-done = f32[3,512]{1,0:T(4,128)S(1)} copy-done((f32[3,512]{1,0:T(4,128)S(1)}, f32[3,512]{1,0:T(4,128)}, u32[]{:S(2)}) %copy-start) | copy-done | bytes 6168
  0.7 55.6 %shard_map.46 = bf16[64,16,512]{2,1,0:T(8,128)(2,1)S(1)} custom-call(f32[3,512]{1,0:T(4,128)S(1)} %copy-done, bf16[1024,512]{1,0:T(8,128)(2,1)} %bitcast.5, bf16[3,512,1536]{2,1,0:T(8,128)(2,1)} %wi_hbm.1, bf16[3,512,512]{2,1,0:T(8,128)(2,1)} %wo_hbm.1), custom_call_target="tpu_custom_call" | custom-call | flops 6442450944 | bytes 4194304 | tf_op jit(solution)/shard_map/pallas_call | solution.py:340
  56.3 1.0 %copy.7 = bf16[64,1,16,512]{3,2,1,0:T(8,128)(2,1)} copy(bf16[64,1,16,512]{3,2,1,0:T(8,128)(2,1)S(1)} %bitcast.4) | data formatting | bytes 2097152
Async XLA Ops:
  0.0 0.7 %copy-start = (f32[3,512]{1,0:T(4,128)S(1)}, f32[3,512]{1,0:T(4,128)}, u32[]{:S(2)}) copy-start(f32[3,512]{1,0:T(4,128)} %gain_hbm.1) | copy-start | bytes 18436

commit v8 on v7

--- a/solution.py
+++ b/solution.py
@@ -149,9 +149,6 @@
     for device in others:
         pl.semaphore_signal(barrier, inc=1, device_id=where(device), device_id_type=MESH)
     bias_ref[0] = mask_of(lambda i: i // frames)
-    bias_ref[1] = mask_of(lambda i: i % PIECE)
-    bias_ref[2] = mask_of(lambda i: (i // half) % some)
-    bias_ref[3] = mask_of(lambda i: i // (rows * short) * short + i % short)
     for copy in x_copies:
         copy.wait()
     for p in range(planes):
@@ -209,6 +206,10 @@
                 send_sem=short_sem.at[2], recv_sem=short_sem.at[part],
                 device_id=where(device), device_id_type=MESH,
             ).start()
+
+    bias_ref[1] = mask_of(lambda i: i % PIECE)
+    bias_ref[2] = mask_of(lambda i: (i // half) % some)
+    bias_ref[3] = mask_of(lambda i: i // (rows * short) * short + i % short)
 
     for k in range(1, early):
         y = along_frames([k], spots)

time: 57.5 us -> 57.5 us (level)
  no operation moved by 1% of the time
where the time goes in v8:
time: 57.5 us; the launch traced here: 57.3 us
  Pallas kernels  55.6 us (97%)
  local copies, waits for them, and re-layouts  1.67 us (3%)
    pallas_call x1, Pallas kernels, kernel_body(): pl.pallas_call(functools.partial(kernel, sizes), out_shape=jax.ShapeDtype...  55.6 us
    unnamed x3, local copies, waits for them, and re-layouts  1.67 us

profile of v8, /device:TPU:0, one launch (start us, length us, event | category | flops | bytes accessed | tf_op | source)
XLA Modules:
  0.0 57.3 jit_solution(15535694857708140712)
XLA Ops:
  0.0 0.0 copy-start
  0.0 0.7 %copy-done = f32[3,512]{1,0:T(4,128)S(1)} copy-done((f32[3,512]{1,0:T(4,128)S(1)}, f32[3,512]{1,0:T(4,128)}, u32[]{:S(2)}) %copy-start) | copy-done | bytes 6168
  0.7 55.6 %shard_map.46 = bf16[64,16,512]{2,1,0:T(8,128)(2,1)S(1)} custom-call(f32[3,512]{1,0:T(4,128)S(1)} %copy-done, bf16[1024,512]{1,0:T(8,128)(2,1)} %bitcast.5, bf16[3,512,1536]{2,1,0:T(8,128)(2,1)} %wi_hbm.1, bf16[3,512,512]{2,1,0:T(8,128)(2,1)} %wo_hbm.1), custom_call_target="tpu_custom_call" | custom-call | flops 6442450944 | bytes 4194304 | tf_op jit(solution)/shard_map/pallas_call | solution.py:341
  56.3 1.0 %copy.7 = bf16[64,1,16,512]{3,2,1,0:T(8,128)(2,1)} copy(bf16[64,1,16,512]{3,2,1,0:T(8,128)(2,1)S(1)} %bitcast.4) | data formatting | bytes 2097152
Async XLA Ops:
  0.0 0.7 %copy-start = (f32[3,512]{1,0:T(4,128)S(1)}, f32[3,512]{1,0:T(4,128)}, u32[]{:S(2)}) copy-start(f32[3,512]{1,0:T(4,128)} %gain_hbm.1) | copy-start | bytes 18436
